TPU v7x, 32 devices: a whole 2x2x4 slice. The times are simulated.
32 devices in a mesh: dp: 8 (over z, y), seq: 4 (over x, core).
Axes of the slice: x: 2, y: 2, z: 4, core: 2. Of those that a mesh axis runs over, the one named last changes fastest.
Arguments:
- long_ids: int32 [24, 512], P('dp', 'seq'), may hold values from 0 to 4100
- long_targets: int32 [24, 512], P('dp', 'seq'), may hold values from 0 to 4100
- long_mask: int32 [24, 512], P('dp', 'seq'), may hold values from 0 to 1
- long_lengths: int32 [24], P('dp'), may hold values from 256 to 512, as said below
- short_ids: int32 [64, 128], P(('dp', 'seq')), may hold values from 0 to 4100
- short_targets: int32 [64, 128], P(('dp', 'seq')), may hold values from 0 to 4100
- short_mask: int32 [64, 128], P(('dp', 'seq')), may hold values from 0 to 1
- short_lengths: int32 [64], P(('dp', 'seq')), may hold values from 64 to 128, as said below
- table: float32 [4101, 768], P(None, ('dp', 'seq')), may hold values from -0.21875 to 0.21875
- position: float32 [512, 768], P(None, ('dp', 'seq')), may hold values from -0.21875 to 0.21875
- qkv_weight: float32 [768, 2304], P(('dp', 'seq')), may hold values from -0.21875 to 0.21875
- out_weight: float32 [768, 768], P(('dp', 'seq')), may hold values from -1.75 to 1.75
- in_weight: float32 [768, 3072], P(('dp', 'seq')), may hold values from -0.21875 to 0.21875
- down_weight: float32 [3072, 768], P(('dp', 'seq')), may hold values from -0.109375 to 0.109375
- norms: float32 [768, 6], P(('dp', 'seq')), may hold values from -1 to 3, as said below
- table_rows: float32 [4101], replicated, may hold values from 1.5875193e-08 to 6.350077e-08
- table_cols: float32 [768], P(('dp', 'seq')), may hold values from 1.5875193e-08 to 6.350077e-08
- position_rows: float32 [512], replicated, may hold values from 2.4283373e-09 to 9.713349e-09
- position_cols: float32 [768], P(('dp', 'seq')), may hold values from 2.4283373e-09 to 9.713349e-09
- qkv_rows: float32 [768], P(('dp', 'seq')), may hold values from 8.477105e-08 to 3.390842e-07
- qkv_cols: float32 [2304], replicated, may hold values from 8.477105e-08 to 3.390842e-07
- out_rows: float32 [768], P(('dp', 'seq')), may hold values from 8.477105e-08 to 3.390842e-07
- out_cols: float32 [768], replicated, may hold values from 8.477105e-08 to 3.390842e-07
- in_rows: float32 [768], P(('dp', 'seq')), may hold values from 8.477105e-08 to 3.390842e-07
- in_cols: float32 [3072], replicated, may hold values from 8.477105e-08 to 3.390842e-07
- down_rows: float32 [3072], P(('dp', 'seq')), may hold values from 8.477105e-08 to 3.390842e-07
- down_cols: float32 [768], replicated, may hold values from 8.477105e-08 to 3.390842e-07
- norm_moment: float32 [768, 6], P(('dp', 'seq')), may hold values from 8.477105e-08 to 3.390842e-07
Outputs:
- loss_sum: float32 [], replicated
- mask_count: float32 [], replicated
- table_grad: float32 [4101, 768], P(None, ('dp', 'seq'))
- position_grad: float32 [512, 768], P(None, ('dp', 'seq'))
- qkv_grad: float32 [768, 2304], P(('dp', 'seq'))
- out_grad: float32 [768, 768], P(('dp', 'seq'))
- in_grad: float32 [768, 3072], P(('dp', 'seq'))
- down_grad: float32 [3072, 768], P(('dp', 'seq'))
- norm_grad: float32 [768, 6], P(('dp', 'seq'))
- table_rows_new: float32 [4101], replicated
- table_cols_new: float32 [768], P(('dp', 'seq'))
- position_rows_new: float32 [512], replicated
- position_cols_new: float32 [768], P(('dp', 'seq'))
- qkv_rows_new: float32 [768], P(('dp', 'seq'))
- qkv_cols_new: float32 [2304], replicated
- out_rows_new: float32 [768], P(('dp', 'seq'))
- out_cols_new: float32 [768], replicated
- in_rows_new: float32 [768], P(('dp', 'seq'))
- in_cols_new: float32 [3072], replicated
- down_rows_new: float32 [3072], P(('dp', 'seq'))
- down_cols_new: float32 [768], replicated
- norm_moment_new: float32 [768, 6], P(('dp', 'seq'))
- table_new: float32 [4101, 768], P(None, ('dp', 'seq'))
- position_new: float32 [512, 768], P(None, ('dp', 'seq'))
- qkv_new: float32 [768, 2304], P(('dp', 'seq'))
- out_new: float32 [768, 768], P(('dp', 'seq'))
- in_new: float32 [768, 3072], P(('dp', 'seq'))
- down_new: float32 [3072, 768], P(('dp', 'seq'))
- norm_new: float32 [768, 6], P(('dp', 'seq'))
Inputs may be any that keep to these rules, and one draw needn't show every extreme that they name: `long_lengths`: in every aligned block of 3 rows one row has length 512. `short_lengths`: in every aligned block of 2 rows one row has length 128. `norms`: columns 0, 2 and 4 are positive gains, columns 1, 3 and 5 shifts.
All inputs are finite; a program needn't handle non-finite values.
Results may differ from a plain program's by a relative error of at most 0.0085.
The roundings to bfloat16 on the way count: a program that leaves them out, or rounds other values in their place, can miss the bound.
Values may be sent and summed in bfloat16 or wider, within the bound.
A program may use at most 192 MiB of HBM per device.

v0:
```python
import functools

import jax
import jax.numpy as jnp
from jax import lax
from jax.experimental import pallas as pl
from jax.experimental.pallas import tpu as pltpu
from jax.sharding import PartitionSpec as P

D = 768
HEADS = 12
HEAD_DIM = 64
VOCAB = 4101
STEP = 10
SPAN = 128

EPSILON = 1e-12
SQUARE_FLOOR = 1e-30
learn_rate = 0.3

MESH = pl.DeviceIdType.MESH
F32 = jnp.float32
BF16 = jnp.bfloat16

NORM_AT = VOCAB
COUNT_AT = VOCAB + 6
TABLE_END = 4352
PLACE_AT = 4608
WIDE = PLACE_AT + 512

SHAPES = ((24, WIDE), (24, 3 * D), (24, D), (24, 4 * D), (96, D))
E_, Q_, O_, I_, D_ = range(5)
CLASS_A, CLASS_B, CLASS_C = (E_, O_), (Q_, D_), (I_,)
UP, DOWN, XWAY, YWAY, SIDE = range(5)


def here():
    dp, seq = lax.axis_index("dp"), lax.axis_index("seq")
    return dp // 2, dp % 2, seq // 2, seq % 2


def device(z, y, x, c):
    return {"dp": z * 2 + y, "seq": x * 2 + c}


def chip(z, y, x):
    return z * 4 + y * 2 + x


def all_peers():
    z, y, x, c = here()
    return (
        device(z + 1, y, x, c),
        device(z - 1, y, x, c),
        device(z, y, 1 - x, c),
        device(z, 1 - y, x, c),
        device(z, y, x, 1 - c),
    )


SUM_AT = (0, WIDE, WIDE + 3 * D, WIDE + 4 * D, WIDE + 8 * D, WIDE + 9 * D)
SUMS = WIDE + 9 * D + 256


def lanes_of(members):
    lane = lax.broadcasted_iota(jnp.int32, (1, 128), 1)
    row = jnp.zeros((1, 128), F32)
    for index, member in enumerate(members):
        row = jnp.where(lane == index, member, row)
    return row


def lane_at(row, index):
    lane = lax.broadcasted_iota(jnp.int32, row.shape, 1)
    return jnp.sum(jnp.where(lane == index, row, 0.0), 1, keepdims=True)


def column_of(row):
    size = row.shape[1]
    diagonal = lax.broadcasted_iota(jnp.int32, (size, size), 0) == lax.broadcasted_iota(
        jnp.int32, (size, size), 1
    )
    return jnp.sum(jnp.where(diagonal, row, 0.0), 1, keepdims=True)


def row_of(column):
    size = column.shape[0]
    diagonal = lax.broadcasted_iota(jnp.int32, (size, size), 0) == lax.broadcasted_iota(
        jnp.int32, (size, size), 1
    )
    return jnp.sum(jnp.where(diagonal, column, 0.0), 0, keepdims=True)


def as_row(ref):
    return ref[...].reshape(1, ref.shape[0])


def total_sum(array):
    return jnp.sum(jnp.sum(array, 1, keepdims=True), 0, keepdims=True)


def sum_everywhere(value, first, second, third, sems):
    z, y, x, c = here()
    spot = y * 2 + x
    side_send, side_recv, plane_send, plane_recv, z_send, z_recv = sems

    def copy(src, dst, send, recv, peer):
        return pltpu.make_async_remote_copy(
            src_ref=src, dst_ref=dst, send_sem=send, recv_sem=recv, device_id=peer, device_id_type=MESH
        )

    first[0] = value
    swap = copy(first.at[0], first.at[1], side_send, side_recv, device(z, y, x, 1 - c))
    swap.start()
    swap.wait_recv()
    second[spot] = first[0] + first[1]
    plane = []
    for i, (to_y, to_x) in enumerate(((y, 1 - x), (1 - y, x), (1 - y, 1 - x))):
        plane.append(
            copy(second.at[spot], second.at[spot], plane_send.at[i], plane_recv.at[i], device(z, to_y, to_x, c))
        )
        plane[i].start()
    for member in plane:
        member.wait_recv()
    third[z] = (second[0] + second[1]) + (second[2] + second[3])
    column = []
    for i in range(3):
        to_z = (z + 1 + i) % 4
        column.append(copy(third.at[z], third.at[z], z_send.at[i], z_recv.at[i], device(to_z, y, x, c)))
        column[i].start()
    for member in column:
        member.wait_recv()
    for member in [swap] + plane + column:
        member.wait_send()
    return (third[0] + third[1]) + (third[2] + third[3])


def gelu_pair(hidden):
    normal_cdf = 0.5 * (1.0 + lax.erf(hidden * 0.7071067811865476))
    return (
        hidden * normal_cdf,
        normal_cdf + hidden * jnp.exp(-0.5 * hidden * hidden) * 0.3989422804014327,
    )


def dot_nn(left, right):
    return jnp.dot(left, right, preferred_element_type=F32)


def dot_nt(left, right):
    return lax.dot_general(left, right, (((1,), (1,)), ((), ())), preferred_element_type=F32)


def dot_tn(left, right):
    return lax.dot_general(left, right, (((0,), (0,)), ((), ())), preferred_element_type=F32)


def at(index, size):
    if isinstance(index, int):
        return pl.ds(index * size, size)
    return pl.ds(pl.multiple_of(index * size, size), size)


def each(count, body):
    def step(index, carry):
        body(index)
        return carry

    lax.fori_loop(0, count, step, 0)


def each_unrolled(count, body):
    for index in range(count):
        body(index)


ROWS = 128
TILE = 256
HALF = 320
TABLE_TILES = TABLE_END // TILE


def head_lanes(first):
    lane = lax.broadcasted_iota(jnp.int32, (1, 128), 1)
    return (lane < HEAD_DIM) if first else (lane >= HEAD_DIM)


def layer_norm(value, gain, shift):
    centred = value - jnp.sum(value, 1, keepdims=True) / D
    inverse = lax.rsqrt(jnp.sum(centred * centred, 1, keepdims=True) / D + EPSILON)
    normed = centred * inverse
    return normed * gain + shift, normed, inverse


def layer_norm_back(grad, normed, inverse, gain):
    scaled = grad * gain
    return inverse * (
        scaled - jnp.sum(scaled, 1, keepdims=True) / D - normed * (jnp.sum(scaled * normed, 1, keepdims=True) / D)
    )


def put_lane(ref, rows, index, value):
    lane = lax.broadcasted_iota(jnp.int32, (1, 128), 1)
    ref[rows, :] = jnp.where(lane == index, value, ref[rows, :])


def set_bias(bias, cols, keys, last):
    same = cols[0:last, 4:5] == keys[1:2, 0:last]
    bias[...] = jnp.where(same & (keys[0:1, 0:last] > 0), 0.0, -1e30)


CHOOSE, EMBED, NORM_A, PROJECT, TURN_X, ATTEND, OUT, NORM_B, FEED_IN, TURN_A, FEED_OUT, REST = range(12)
FRONT = (
    67, 35, 36, 66, 32, 64, 100, 131, 1000, 69, 39, 1, 108, 161, 68, 33, 164, 73, 34, 4,
    99, 65, 71, 43, 50, 40, 75, 38, 3, 130, 162, 163, 160, 37, 6, 79, 172, 2, 0, 70,
    46, 96, 8, 76, 98, 166, 165, 44, 41, 169, 83, 42, 80, 74, 97, 175, 72, 47, 5, 129,
    78, 13, 170, 48, 10, 7, 168, 1001, 45, 132, 16, 104, 51, 82, 81, 49, 77, 174, 12, 1016,
    1017, 1018, 128, 18, 9, 11, 102, 1019, 1020, 1021, 103, 17, 1032, 177, 15, 14, 19, 173, 101, 167,
    109, 176, 135, 136, 1048, 1049, 1050, 1051, 1052, 1053, 1054, 1055, 133, 1056, 1064, 1080, 107, 1081, 171, 1082,
    106, 114, 1083, 105, 112, 1084, 178, 137, 134, 146, 179, 115, 142, 1085, 113, 141, 140, 1096, 1097, 1098,
    110, 111, 139, 1112, 1128, 1129, 1130, 138, 1131, 1132, 1133, 1134, 1135, 1136, 147, 144, 143, 145, 1137, 1138,
    1139, 1160, 1161, 1162, 1176,
)


def front_hooks():
    hooks, before = {}, []
    for task in FRONT:
        if task < 1000:
            before.append(task)
        else:
            hooks[((task - 1000) // 16, (task - 1000) % 16)] = before
            before = []
    return hooks


def front_kernel(*refs):
    raw, (long_len, short_len) = refs[0:13], refs[13:15]
    count_out, gains_out, side, cols, keys, squares = refs[15:21]
    x_t, mix_out, a_out, act_out, y_out, slope_out, qkv_out, na_out = refs[21:29]
    nb_outs, nc_outs, weight_outs = refs[29:31], refs[31:33], refs[33:38]
    wide, qkv_w, out_w, in_w, down_w = weights = refs[38:43]
    value, na, low_a, low_y, mix, qkv, act, slope, pick, pick_two, bias, turned = refs[43:55]
    nb, nc = refs[55:57], refs[57:59]
    held, wide_shard, merge, pieces, land = refs[59:72], refs[72], refs[73:78], refs[78], refs[79]
    raw_sem, swap_send, swap_recv, token_send, token_recv, send_sem, link_recv, side_recv = refs[80:88]
    out_sem, turn_sem = refs[88:90]
    z, y, x, c = here()
    peers = all_peers()
    me = chip(z, y, x)
    seq = x * 2 + c
    alone = seq // 3
    tokens = value.shape[0]
    last = tokens - SPAN
    hooks = front_hooks()

    barrier = pltpu.get_barrier_semaphore()
    cross = device(z, y, 1 - x, 1 - c)
    column = [device((z + 1 + i) % 4, y, x, c) for i in range(3)]
    for peer in [peers[XWAY], peers[YWAY], peers[SIDE], cross] + column:
        pl.semaphore_signal(barrier, inc=1, device_id=peer, device_id_type=MESH)
    raws = [pltpu.make_async_copy(raw[i], held[i], raw_sem.at[i]) for i in range(13)]
    for member in raws:
        member.start()
    for member in raws:
        member.wait()
    long_ids, long_targets, long_mask, short_ids, short_targets, short_mask, tall, place, qkv_s, out_s, in_s, down_s, norms = held

    pieces[...] = jnp.zeros(pieces.shape, jnp.int32)
    land[4] = jnp.zeros((8, SPAN), jnp.int32)
    lane = lax.broadcasted_iota(jnp.int32, (1, SPAN), 1)
    count = jnp.zeros((1, SPAN), jnp.int32)
    for t in range(5):
        if t < 3:
            ids, targets, mask = long_ids[t : t + 1, :], long_targets[t : t + 1, :], long_mask[t : t + 1, :]
            keep = (lane + seq * SPAN < long_len[t]).astype(jnp.int32)
        else:
            row = (1, 0)[t - 3]
            ids, targets, mask = (member[row : row + 1, :] for member in (short_ids, short_targets, short_mask))
            keep = (lane < short_len[row]).astype(jnp.int32)
        target = pieces.at[t] if t < 4 else land.at[4]
        target[0:1, :] = ids
        target[2:3, :] = targets
        target[3:4, :] = mask * keep
        target[5:6, :] = keep
        count = count + mask * keep
    count = jnp.sum(count.astype(F32), 1, keepdims=True)
    high = jnp.floor(count * (1.0 / 256.0))

    wide_shard[:, 0:4096] = tall[:, 0:4096]
    edge = jnp.zeros((24, 128), F32)
    tile_lane = lax.broadcasted_iota(jnp.int32, (24, 128), 1)
    tall_edge = tall[:, 4096:VOCAB]
    members = [lane_at(tall_edge, i) for i in range(VOCAB - 4096)]
    members += [column_of(norms[i : i + 1, :]) for i in range(6)]
    members += [high, count - high * 256.0]
    for i, member in enumerate(members):
        edge = jnp.where(tile_lane == i, member, edge)
    wide_shard[:, 4096:4224] = edge
    wide_shard[:, 4224:PLACE_AT] = jnp.zeros((24, PLACE_AT - 4224), F32)
    wide_shard[:, PLACE_AT:] = place[...]
    shards = (wide_shard, qkv_s, out_s, in_s, down_s)

    pl.semaphore_wait(barrier, 7)
    swaps = []
    for m in (E_, Q_, I_, D_, O_):
        size, half = SHAPES[m][0], SHAPES[m][1] // 2
        swaps.append(
            pltpu.make_async_remote_copy(
                src_ref=shards[m].at[:, pl.ds(pl.multiple_of((1 - c) * half, 128), half)],
                dst_ref=merge[m].at[pl.ds(pl.multiple_of(c * size, 8), size), :],
                send_sem=swap_send.at[m],
                recv_sem=swap_recv.at[m],
                device_id=peers[SIDE],
                device_id_type=MESH,
            )
        )
        swaps[-1].start()
    token_copies = []
    for i, (to_x, to_c) in enumerate(((x, 1 - c), (1 - x, c), (1 - x, 1 - c))):
        token_copies.append(
            pltpu.make_async_remote_copy(
                src_ref=pieces.at[to_x * 2 + to_c],
                dst_ref=land.at[seq],
                send_sem=token_send.at[i],
                recv_sem=token_recv.at[i],
                device_id=device(z, y, to_x, to_c),
                device_id_type=MESH,
            )
        )
        token_copies[-1].start()
    land[seq] = pieces[seq]

    def part(piece, k, half):
        m, skip, wide_part = PIECES[piece]
        size = 2 * SHAPES[m][0]
        start = pl.multiple_of(half * (SHAPES[m][1] // 2) + skip, 128)
        return weights[m].at[pl.ds(pl.multiple_of(k * size, size), size), pl.ds(start, wide_part)]

    FIRST_WAY, SECOND_WAY, SIDE_WAY = 0, 1, 2

    def copy_of(piece, k, way):
        ways = (XWAY, YWAY) if piece in Y_FIRST else (YWAY, XWAY)
        peer = column[way - 3] if way > 2 else peers[SIDE] if way == SIDE_WAY else peers[ways[way]]
        return pltpu.make_async_remote_copy(
            src_ref=part(piece, k, c),
            dst_ref=part(piece, k, c),
            send_sem=send_sem.at[piece, k, way],
            recv_sem=(side_recv if way == SIDE_WAY else link_recv).at[piece, k],
            device_id=peer,
            device_id_type=MESH,
        )

    def block_of(number):
        piece, task = number // 32, number % 32
        last_y = piece in Y_FIRST
        if task < 5:
            return piece, me, (3 + task if task < 3 else FIRST_WAY if task == 3 else SECOND_WAY,), False
        if task < 8:
            return piece, chip((z + task - 4) % 4, y, x), (FIRST_WAY, SECOND_WAY, SIDE_WAY), True
        if task < 12:
            t = (z + task - 8) % 4
            return piece, chip(t, y, 1 - x) if last_y else chip(t, 1 - y, x), (SECOND_WAY, SIDE_WAY), True
        t, other = (z + (task - 12) // 2) % 4, (task - 12) % 2
        if last_y:
            return piece, chip(t, 1 - y, 1 - x if other else x), (SIDE_WAY,), True
        return piece, chip(t, 1 - y if other else y, 1 - x), (SIDE_WAY,), True

    def transfer(number):
        piece, k, ways, waits = block_of(number)
        if waits:
            copy_of(piece, k, FIRST_WAY).wait_recv()
        for way in ways:
            copy_of(piece, k, way).start()

    def before(step, index, base=0):
        for (name, part_index), tasks in hooks.items():
            part_index = part_index - base
            if name != step or not tasks or (step == EMBED and not 0 <= part_index < 3):
                continue
            if index is None or isinstance(index, int):
                if part_index == (index or 0):
                    for number in tasks:
                        transfer(number)
            else:

                @pl.when(index == part_index)
                def _(tasks=tasks):
                    for number in tasks:
                        transfer(number)

    def need(*wanted):
        for piece in wanted:
            for k in range(16):
                pltpu.make_async_remote_copy(
                    src_ref=part(piece, k, 1 - c),
                    dst_ref=part(piece, k, 1 - c),
                    send_sem=send_sem.at[piece, k, SIDE_WAY],
                    recv_sem=side_recv.at[piece, k],
                    device_id=peers[SIDE],
                    device_id_type=MESH,
                ).wait_recv()

    for number, m in enumerate((E_, Q_, I_, D_, O_)):
        swaps[number].wait_recv()
        size, half = SHAPES[m][0], SHAPES[m][1] // 2
        merge[m][pl.ds(pl.multiple_of(c * size, 8), size), :] = shards[m][:, pl.ds(pl.multiple_of(c * half, 128), half)]
        rows = pl.ds(pl.multiple_of(me * 2 * size, 2 * size), 2 * size)
        weights[m][rows, pl.ds(pl.multiple_of(c * half, 128), half)] = merge[m][...].astype(BF16)
        for piece in range(6):
            if PIECES[piece][0] == m:
                copy_of(piece, me, SIDE_WAY).start()
    for copy in token_copies:
        copy.wait_recv()
    side[...] = jnp.zeros(side.shape, F32)
    keys[...] = jnp.zeros(keys.shape, jnp.int32)
    zeros = jnp.zeros((1, SPAN), F32)
    for b in range(5):
        tile = land[b]
        shift = b * SPAN * (1 - alone) if b < 4 else 0
        row = b * alone if b < 4 else 4
        spot = (lane + shift + PLACE_AT).astype(F32)
        row_lane = (lane * 0 + row).astype(F32)
        ids, targets, weight = (tile[i : i + 1].astype(F32) for i in (0, 2, 3))
        stacked = jnp.concatenate((ids, spot, targets, weight, row_lane, zeros, zeros, zeros), 0)
        stacked = jnp.concatenate((stacked, jnp.zeros((120, SPAN), F32)), 0)
        cols[b * SPAN : (b + 1) * SPAN, :] = stacked.T.astype(jnp.int32)
        keys[0:1, b * SPAN : (b + 1) * SPAN] = tile[5:6]
        keys[1:2, b * SPAN : (b + 1) * SPAN] = lane * 0 + row
        keys[2:4, b * SPAN : (b + 1) * SPAN] = tile[2:4]
    set_bias(bias, cols, keys, last)
    found = [total_sum(member[...] * member[...]) for member in (tall, place, qkv_s, out_s, in_s, down_s)]
    norm_squares = jnp.sum(norms[...] * norms[...], 1, keepdims=True)
    squares[...] = lanes_of(found + [norm_squares[i : i + 1] for i in range(6)])

    turns, outs = {}, {}

    def turn_out(source, target, slot):
        if slot in turns:
            turns[slot].wait()

        def some(index):
            turned[slot, :, at(index, ROWS)] = source[at(index, ROWS), :].T

        each(tokens // ROWS, some)
        turns[slot] = pltpu.make_async_copy(turned.at[slot], target, turn_sem.at[slot])
        turns[slot].start()

    def put_out(name, source, target):
        outs[name] = pltpu.make_async_copy(source, target, out_sem.at[len(outs)])
        outs[name].start()

    picks = (pick, pick_two)
    halves = [pl.ds(half * HALF, HALF) for half in range(2)]
    for half in range(2):

        def choose(index):
            column_lane = lax.broadcasted_iota(jnp.int32, (1, TILE), 1) + index * TILE
            hit = (cols[halves[half], 0:1] == column_lane) | (cols[halves[half], 1:2] == column_lane)
            picks[half][:, at(index, TILE)] = jnp.where(hit, 1.0, 0.0).astype(BF16)

        before(CHOOSE, half)
        each(WIDE // TILE, choose)

    before(EMBED, 0)
    hooks.pop((EMBED, 0))
    need(1, 2)
    put_out("wide", wide, weight_outs[4])
    for half in range(2):

        def embed(index):
            before(EMBED, index, half * 3)
            value[halves[half], at(index, TILE)] = dot_nt(picks[half][...], wide[at(index, TILE), :])

        each_unrolled(D // TILE, embed)

    gains = wide[:, 4096:4224].astype(F32).T
    gains_out[...] = gains[0:16]
    counts = jnp.sum(gains[11:13], 1, keepdims=True) / 24.0
    mask_count = counts[0:1] * 256.0 + counts[1:2]
    count_out[...] = mask_count
    norm_rows = [gains_out[5 + i : 6 + i, :] for i in range(6)]
    before(NORM_A, None)

    def norm_a(index):
        rows = at(index, ROWS)
        found, normed, inverse = layer_norm(value[rows, :], norm_rows[0], norm_rows[1])
        value[rows, :] = found
        low_a[rows, :] = found.astype(BF16)
        na[rows, :] = normed
        put_lane(side, rows, 12, inverse)

    each(tokens // ROWS, norm_a)
    put_out("na", na, na_out)
    before(PROJECT, 0)
    need(0)

    def project(index):
        before(PROJECT, index)
        qkv[:, at(index, TILE)] = dot_nn(low_a[...], qkv_w[:, at(index, TILE)]).astype(BF16)

    hooks.pop((PROJECT, 0))
    each_unrolled(3 * D // TILE, project)
    put_out("qkv", qkv, qkv_out)
    put_out("qkv_w", qkv_w, weight_outs[0])
    before(TURN_X, None)
    turn_out(low_a, x_t, 0)

    def attend_pair(pair):
        before(ATTEND, pair)
        for start, size in ((0, last), (last, SPAN)):
            rows = pl.ds(start, size)
            query = qkv[rows, at(pair, 128)]
            key = qkv[rows, pl.ds(pl.multiple_of(D + pair * 128, 128), 128)]
            val = qkv[rows, pl.ds(pl.multiple_of(2 * D + pair * 128, 128), 128)]
            mask = bias[...] if start == 0 else jnp.where(keys[0:1, last:tokens] > 0, 0.0, -1e30)
            mixed = []
            for first in (True, False):
                chosen = jnp.where(head_lanes(first), query, jnp.zeros_like(query))
                scores = dot_nt(chosen, key) * 0.125 + mask
                highest = jnp.max(scores, 1, keepdims=True)
                raised = jnp.exp(scores - highest)
                summed = jnp.sum(raised, 1, keepdims=True)
                shares = (raised * (1.0 / summed)).astype(BF16)
                mixed.append(dot_nn(shares, val))
                put_lane(side, rows, 2 * pair + (0 if first else 1), highest + jnp.log(summed))
            mix[rows, at(pair, 128)] = jnp.where(head_lanes(True), mixed[0], mixed[1]).astype(BF16)

    each(HEADS // 2, attend_pair)
    before(OUT, 0)
    hooks.pop((OUT, 0))
    need(5)

    def out_project(index):
        before(OUT, index)
        value[:, at(index, TILE)] = value[:, at(index, TILE)] + dot_nn(mix[...], out_w[:, at(index, TILE)])

    each_unrolled(D // TILE, out_project)
    put_out("out_w", out_w, weight_outs[1])
    put_out("mix", mix, mix_out)
    before(NORM_B, None)

    def norm_b(index):
        rows = at(index, ROWS)
        found, normed, inverse = layer_norm(value[rows, :], norm_rows[2], norm_rows[3])
        value[rows, :] = found
        low_y[rows, :] = found.astype(BF16)
        nb[0][rows, :], nb[1][rows, :] = split_two(normed)
        put_lane(side, rows, 13, inverse)

    each(tokens // ROWS, norm_b)
    put_out("a", low_y, a_out)
    put_out("nb0", nb[0], nb_outs[0])
    put_out("nb1", nb[1], nb_outs[1])
    before(FEED_IN, 0)
    hooks.pop((FEED_IN, 0))
    need(3)

    def feed_in(index):
        before(FEED_IN, index)
        hidden = dot_nn(low_y[...], in_w[:, at(index, TILE)])
        active, slant = gelu_pair(hidden)
        active = active.astype(BF16)
        act[:, at(index, TILE)] = active
        slope[:, at(index, TILE)] = slant.astype(BF16)

    each_unrolled(4 * D // TILE, feed_in)
    put_out("act", act, act_out)
    put_out("slope", slope, slope_out)
    put_out("in_w", in_w, weight_outs[2])
    before(TURN_A, None)
    before(FEED_OUT, 0)
    hooks.pop((FEED_OUT, 0))
    need(4)

    def feed_out(index):
        before(FEED_OUT, index)
        value[:, at(index, TILE)] = value[:, at(index, TILE)] + dot_nn(act[...], down_w[:, at(index, TILE)])

    each_unrolled(D // TILE, feed_out)
    put_out("down_w", down_w, weight_outs[3])
    before(REST, None)
    turns[0].wait()

    def norm_c(index):
        rows = at(index, ROWS)
        found, normed, inverse = layer_norm(value[rows, :], norm_rows[4], norm_rows[5])
        low_a[rows, :] = found.astype(BF16)
        nc[0][rows, :], nc[1][rows, :] = split_two(normed)
        put_lane(side, rows, 14, inverse)

    each(tokens // ROWS, norm_c)
    put_out("y", low_a, y_out)
    put_out("nc0", nc[0], nc_outs[0])
    put_out("nc1", nc[1], nc_outs[1])
    for swap in swaps:
        swap.wait_send()
    for copy in token_copies:
        copy.wait_send()
    for piece in range(6):
        copy_of(piece, me, SIDE_WAY).wait_send()
    for number in FRONT:
        if number < 1000:
            piece, k, ways, _ = block_of(number)
            for way in ways:
                copy_of(piece, k, way).wait_send()
    for copy in outs.values():
        copy.wait()


def front(large, lengths):
    vmem, hbm = pl.BlockSpec(memory_space=pltpu.VMEM), pl.BlockSpec(memory_space=pl.ANY)
    smem = pl.BlockSpec(memory_space=pltpu.SMEM)
    shape, dma = jax.ShapeDtypeStruct, pltpu.SemaphoreType.DMA
    tokens = 5 * SPAN
    small = [shape((1, 1), F32), shape((16, D), F32), shape((tokens, 128), F32)]
    small += [shape((tokens, 128), jnp.int32), shape((8, tokens), jnp.int32), shape((1, 128), F32)]
    out = [shape((D, tokens), BF16)] + [shape((tokens, width), BF16) for width in (D, D, 4 * D, D, 4 * D, 3 * D)]
    out += [shape((tokens, D), F32)] + [shape((tokens, D), BF16)] * 4
    out += [shape((32 * SHAPES[m][0], SHAPES[m][1]), BF16) for m in (Q_, O_, I_, D_, E_)]
    return pl.pallas_call(
        front_kernel,
        out_shape=small + out,
        in_specs=[hbm] * 13 + [smem] * 2,
        out_specs=[vmem] * len(small) + [hbm] * len(out),
        scratch_shapes=[pltpu.VMEM((32 * size, wide), BF16) for size, wide in SHAPES]
        + [pltpu.VMEM((tokens, D), F32)] * 2
        + [pltpu.VMEM((tokens, D), BF16)] * 3
        + [
            pltpu.VMEM((tokens, 3 * D), BF16),
            pltpu.VMEM((tokens, 4 * D), BF16),
            pltpu.VMEM((tokens, 4 * D), BF16),
            pltpu.VMEM((HALF, WIDE), BF16),
            pltpu.VMEM((HALF, WIDE), BF16),
            pltpu.VMEM((tokens - SPAN, tokens - SPAN), F32),
            pltpu.VMEM((1, D, tokens), BF16),
        ]
        + [pltpu.VMEM((tokens, D), BF16)] * 4
        + [pltpu.VMEM(member.shape, member.dtype) for member in large]
        + [pltpu.VMEM(SHAPES[E_], F32)]
        + [pltpu.VMEM((2 * size, wide // 2), F32) for size, wide in SHAPES]
        + [pltpu.VMEM((4, 8, SPAN), jnp.int32), pltpu.VMEM((5, 8, SPAN), jnp.int32)]
        + [dma((13,)), dma((5,)), dma((5,)), dma((3,)), dma((3,)), dma((6, 16, 6)), dma((6, 16)), dma((6, 16))]
        + [dma((18,)), dma((1,))],
        compiler_params=pltpu.CompilerParams(
            collective_id=0, has_side_effects=True, vmem_limit_bytes=63 * 1024 * 1024
        ),
    )(*large, *lengths)


PACK = 256


def split_two(value):
    high = value.astype(BF16)
    return high, (value - high.astype(F32)).astype(BF16)


def middle_kernel(*refs):
    (wide_h, qkv_wh, out_wh, in_wh, down_h, y_h, act_h, a_h, mix_h, slope_h, qkv_h, na_h) = refs[0:12]
    nb_h, nc_h = refs[12:14], refs[14:16]
    cols, keys, side, gains, count = refs[16:21]
    loss_out, norm_out = refs[21:23]
    glog_out, y_t, a_t, mix_t, act_t, ge_t, gffn_out, gh_out, gattn_out, gqkv_out = refs[23:33]
    wide, qkv_w, out_w, in_w, plain, qkv, na = refs[33:40]
    nb, nc = refs[40:42], refs[42:44]
    slope_ring, act_ring, down_ring = refs[44:47]
    logits, glog, gh, gffn, gattn, gatt, packed, grad, turned, act_turned = refs[47:57]
    back_kv, gqkv, whole_grad, pick, pick_t, bias, side_pack, dq, ge = refs[57:66]
    load_sem, ring_sem, out_sem = refs[66:69]
    tokens = cols.shape[0]
    names = ("wide", "y", "nc0", "nc1", "in_w", "nb0", "nb1", "out_w", "qkv", "qkv_w", "na")
    sources = (wide_h, y_h, nc_h[0], nc_h[1], in_wh, nb_h[0], nb_h[1], out_wh, qkv_h, qkv_wh, na_h)
    targets = (wide, plain, nc[0], nc[1], in_w, nb[0], nb[1], out_w, qkv, qkv_w, na)
    loads = {}
    for i, name in enumerate(names):
        if name != "y":
            loads[name] = pltpu.make_async_copy(sources[i], targets[i], load_sem.at[i])
            loads[name].start()

    weight_row = keys[3:4, :].astype(F32)
    weight_col = cols[:, 3:4].astype(F32)
    earlier = lax.broadcasted_iota(jnp.int32, (tokens, tokens), 0) < lax.broadcasted_iota(jnp.int32, (tokens, tokens), 1)
    later = lax.broadcasted_iota(jnp.int32, (tokens, tokens), 0) > lax.broadcasted_iota(jnp.int32, (tokens, tokens), 1)
    rank_row = dot_nn(
        jnp.broadcast_to(weight_row, (16, tokens)).astype(BF16), jnp.where(earlier, 1.0, 0.0).astype(BF16)
    )[0:1]
    rank_col = dot_nn(
        jnp.where(later, 1.0, 0.0).astype(BF16), jnp.broadcast_to(weight_col, (tokens, 128)).astype(BF16)
    )[:, 0:1]
    rank_row = jnp.where(weight_row > 0, rank_row, -1.0)
    rank_col = jnp.where(weight_col > 0, rank_col, -1.0)
    blocks = (jnp.sum(weight_row).astype(jnp.int32) + (PACK - 1)) // PACK
    blocks = jnp.maximum(blocks, 1)
    inverse_count = 1.0 / count[...]
    norm_rows = [gains[5 + i : 6 + i, :] for i in range(6)]
    loss_out[...] = jnp.zeros((1, 1), F32)
    norm_out[...] = jnp.zeros(norm_out.shape, F32)
    back_kv[...] = jnp.zeros(back_kv.shape, F32)
    whole_grad[...] = jnp.zeros(whole_grad.shape, F32)
    gqkv[:, 0:D] = jnp.zeros((tokens, D), BF16)
    side_first = side[...].astype(BF16)
    rest = side[...] - side_first.astype(F32)
    side_second = rest.astype(BF16)
    side_third = (rest - side_second.astype(F32)).astype(BF16)
    waited = set()

    def load_plain(source):
        return pltpu.make_async_copy(source, plain, load_sem.at[1])

    def ring(kind, source, target):
        def copy(j):
            piece = source.at[at(j, TILE), :] if kind == 2 else source.at[:, at(j, TILE)]
            return pltpu.make_async_copy(piece, target.at[j % 2], ring_sem.at[kind * 2 + j % 2])

        return copy

    rings = [ring(0, slope_h, slope_ring), ring(1, act_h, act_ring), ring(2, down_h, down_ring)]
    outs = [
        (glog, glog_out, 0),
        (turned.at[0], y_t, 1),
        (turned.at[1], a_t, 1),
        (turned.at[2], mix_t, 1),
        (act_turned, act_t, 1),
        (gffn, gffn_out, 0),
        (gh, gh_out, 0),
        (gattn, gattn_out, 0),
    ]

    def out_copy(i, block):
        source, target, axis = outs[i]
        place = at(block, PACK)
        return pltpu.make_async_copy(
            source, target.at[place, :] if axis == 0 else target.at[:, place], out_sem.at[i]
        )

    def wait_load(name):
        loads[name].wait()

    load_plain(y_h).start()
    for name in names:
        if name in ("wide", "nc0", "nc1"):
            wait_load(name)

    def block_step(block, carry):
        slot_col = lax.broadcasted_iota(jnp.int32, (PACK, 1), 0).astype(F32) + (block * PACK).astype(F32)
        slot_row = lax.broadcasted_iota(jnp.int32, (1, PACK), 1).astype(F32) + (block * PACK).astype(F32)
        hit = jnp.where(rank_row == slot_col, 1.0, 0.0)
        pick[...] = hit.astype(BF16)
        pick_t[...] = jnp.where(rank_col == slot_row, 1.0, 0.0).astype(BF16)
        target = jnp.sum(hit * keys[2:3, :].astype(F32), 1, keepdims=True)
        row_of_token = jnp.sum(hit * keys[1:2, :].astype(F32), 1, keepdims=True)
        weight = jnp.sum(hit, 1, keepdims=True)
        bias[...] = jnp.where(
            (row_of_token == keys[1:2, :].astype(F32)) & (keys[0:1, :] > 0), 0.0, -1e30
        )
        side_pack[...] = (
            dot_nn(pick[...], side_first) + dot_nn(pick[...], side_second) + dot_nn(pick[...], side_third)
        )
        for kind in range(3):
            for j in range(2):
                rings[kind](j).start()
        load_plain(y_h).wait()
        packed[...] = dot_nn(pick[...], plain[...]).astype(BF16)
        load_plain(a_h).start()
        turned[0] = packed[...].T
        out_copy(1, block).start()

        def lanes(index):
            return (lax.broadcasted_iota(jnp.int32, (1, TILE), 1) + index * TILE).astype(F32)

        highest = jnp.full((PACK, 128), -1e30, F32)
        for index in range(TABLE_TILES):
            found = dot_nn(packed[...], wide[:, at(index, TILE)])
            if index == TABLE_TILES - 1:
                found = jnp.where(lanes(index) < VOCAB, found, -1e30)
            logits[:, at(index, TILE)] = found
            highest = jnp.maximum(highest, jnp.maximum(found[:, 0:128], found[:, 128:256]))
        highest = jnp.max(highest, 1, keepdims=True)
        summed, picked = jnp.zeros((PACK, 128), F32), jnp.zeros((PACK, 128), F32)
        for index in range(TABLE_TILES):
            found = logits[:, at(index, TILE)]
            raised = jnp.exp(found - highest)
            logits[:, at(index, TILE)] = raised
            own = jnp.where(lanes(index) == target, found, 0.0)
            summed = summed + raised[:, 0:128] + raised[:, 128:256]
            picked = picked + own[:, 0:128] + own[:, 128:256]
        summed = jnp.sum(summed, 1, keepdims=True)
        picked = jnp.sum(picked, 1, keepdims=True)
        loss_out[...] = loss_out[...] + jnp.sum(weight * (highest + jnp.log(summed) - picked), 0, keepdims=True)
        scale = weight * inverse_count
        share = scale / summed
        for index in range(TABLE_TILES):
            found = logits[:, at(index, TILE)] * share - jnp.where(lanes(index) == target, scale, 0.0)
            glog[:, at(index, TILE)] = found.astype(BF16)
        out_copy(0, block).start()
        for index in range(D // TILE):
            grad[:, at(index, TILE)] = dot_nt(glog[...], wide[at(index, TILE), 0:TABLE_END])
        normed = dot_nn(pick[...], nc[0][...]) + dot_nn(pick[...], nc[1][...])
        found = grad[...]
        back = layer_norm_back(found, normed, lane_at(side_pack[...], 14), norm_rows[4])
        norm_out[4:5, :] = norm_out[4:5, :] + jnp.sum(found * normed, 0, keepdims=True)
        norm_out[5:6, :] = norm_out[5:6, :] + jnp.sum(found, 0, keepdims=True)
        grad[...] = back
        gffn[...] = back.astype(BF16)
        out_copy(5, block).start()

        load_plain(a_h).wait()
        turned[1] = dot_nn(pick[...], plain[...]).astype(BF16).T
        out_copy(2, block).start()
        load_plain(mix_h).start()
        for index in range(4 * D // TILE):
            for kind in range(3):
                rings[kind](index).wait()
            slant = dot_nn(pick[...], slope_ring[index % 2])
            found = dot_nt(gffn[...], down_ring[index % 2]) * slant
            gh[:, at(index, TILE)] = found.astype(BF16)
            act_turned[at(index, TILE), :] = dot_nn(pick[...], act_ring[index % 2]).astype(BF16).T
            if index + 2 < 4 * D // TILE:
                for kind in range(3):
                    rings[kind](index + 2).start()
        out_copy(6, block).start()
        out_copy(4, block).start()
        load_plain(mix_h).wait()
        turned[2] = dot_nn(pick[...], plain[...]).astype(BF16).T
        out_copy(3, block).start()
        load_plain(y_h).start()

        @pl.when(block == 0)
        def _():
            for name in names[4:8]:
                wait_load(name)

        for index in range(D // TILE):
            grad[:, at(index, TILE)] = grad[:, at(index, TILE)] + dot_nt(gh[...], in_w[at(index, TILE), :])
        normed = dot_nn(pick[...], nb[0][...]) + dot_nn(pick[...], nb[1][...])
        found = grad[...]
        back = layer_norm_back(found, normed, lane_at(side_pack[...], 13), norm_rows[2])
        norm_out[2:3, :] = norm_out[2:3, :] + jnp.sum(found * normed, 0, keepdims=True)
        norm_out[3:4, :] = norm_out[3:4, :] + jnp.sum(found, 0, keepdims=True)
        gattn[...] = back.astype(BF16)
        out_copy(7, block).start()
        high, low = split_two(back)
        whole_grad[...] = whole_grad[...] + dot_nn(pick_t[...], high) + dot_nn(pick_t[...], low)
        for index in range(D // TILE):
            gatt[:, at(index, TILE)] = dot_nt(gattn[...], out_w[at(index, TILE), :]).astype(BF16)

        @pl.when(block == 0)
        def _():
            wait_load("qkv")

        def attend_pair_back(pair):
            spots = [pl.ds(pl.multiple_of(i * D + pair * 128, 128), 128) for i in range(3)]
            query = dot_nn(pick[...], qkv[:, spots[0]]).astype(BF16)
            key, val = qkv[:, spots[1]], qkv[:, spots[2]]
            given = gatt[:, at(pair, 128)]
            found = []
            for first in (True, False):
                lanes_here = head_lanes(first)
                chosen = jnp.where(lanes_here, query, jnp.zeros_like(query))
                mine = jnp.where(lanes_here, given, jnp.zeros_like(given))
                total = lane_at(side_pack[...], 2 * pair + (0 if first else 1))
                shares = jnp.exp(dot_nt(chosen, key) * 0.125 + bias[...] - total)
                grad_share = dot_nt(mine, val)
                middle = jnp.sum(shares * grad_share, 1, keepdims=True)
                grad_score = (shares * (grad_share - middle)).astype(BF16)
                found.append(
                    (
                        dot_nn(grad_score, key) * 0.125,
                        dot_tn(grad_score, query) * 0.125,
                        dot_tn(shares.astype(BF16), given),
                    )
                )
            lanes_here = head_lanes(True)
            dq[:, at(pair, 128)] = jnp.where(lanes_here, found[0][0], found[1][0]).astype(BF16)
            for i in (1, 2):
                spot = pl.ds(pl.multiple_of((i - 1) * D + pair * 128, 128), 128)
                back_kv[:, spot] = back_kv[:, spot] + jnp.where(lanes_here, found[0][i], found[1][i])

        each(HEADS // 2, attend_pair_back)
        gqkv[:, 0:D] = (gqkv[:, 0:D].astype(F32) + dot_nn(pick_t[...], dq[...])).astype(BF16)
        for i in range(len(outs)):
            out_copy(i, block).wait()
        return carry

    lax.fori_loop(0, blocks, block_step, 0)
    load_plain(y_h).wait()
    gqkv[:, D:] = back_kv[...].astype(BF16)
    copy_qkv = pltpu.make_async_copy(gqkv, gqkv_out, out_sem.at[8])
    copy_qkv.start()
    for ref in (glog, gffn, gh, gattn):
        ref[...] = jnp.zeros(ref.shape, BF16)
    for block in range(1, 3):

        @pl.when(blocks <= block)
        def _():
            for i in range(len(outs)):
                out_copy(i, block).start()

    for name in names[9:]:
        wait_load(name)
    for index in range(D // TILE):
        whole_grad[:, at(index, TILE)] = whole_grad[:, at(index, TILE)] + dot_nt(gqkv[...], qkv_w[at(index, TILE), :])
    zero = jnp.zeros((1, D), F32)

    def norm_a_back(index, carry):
        gain, shift = carry
        rows = at(index, ROWS)
        inverse = lane_at(side[rows, :], 12)
        found, normed = whole_grad[rows, :], na[rows, :]
        ge[:, rows] = layer_norm_back(found, normed, inverse, norm_rows[0]).astype(BF16).T
        return gain + jnp.sum(found * normed, 0, keepdims=True), shift + jnp.sum(found, 0, keepdims=True)

    gain, shift = lax.fori_loop(0, tokens // ROWS, norm_a_back, (zero, zero))
    norm_out[0:1, :] = gain
    norm_out[1:2, :] = shift
    copy_ge = pltpu.make_async_copy(ge, ge_t, out_sem.at[9])
    copy_ge.start()
    for block in range(1, 3):

        @pl.when(blocks <= block)
        def _():
            for i in range(len(outs)):
                out_copy(i, block).wait()

    copy_qkv.wait()
    copy_ge.wait()


def middle(large, small):
    tokens = 5 * SPAN
    slots = 3 * PACK
    vmem, hbm = pl.BlockSpec(memory_space=pltpu.VMEM), pl.BlockSpec(memory_space=pl.ANY)
    shape, dma = jax.ShapeDtypeStruct, pltpu.SemaphoreType.DMA
    out = [shape((slots, TABLE_END), BF16)] + [shape((D, slots), BF16)] * 3 + [shape((4 * D, slots), BF16)]
    out += [shape((D, tokens), BF16), shape((slots, D), BF16), shape((slots, 4 * D), BF16), shape((slots, D), BF16)]
    out += [shape((tokens, 3 * D), BF16)]

    def rows(count, width, kind=BF16):
        return pltpu.VMEM((count, width), kind)

    scratch = [rows(D, WIDE), rows(D, 3 * D), rows(D, D), rows(D, 4 * D), rows(tokens, D), rows(tokens, 3 * D)]
    scratch += [rows(tokens, D, F32)] + [rows(tokens, D)] * 4
    scratch += [pltpu.VMEM((2, tokens, TILE), BF16)] * 2 + [pltpu.VMEM((2, TILE, D), BF16)]
    scratch += [rows(PACK, TABLE_END, F32), rows(PACK, TABLE_END), rows(PACK, 4 * D)] + [rows(PACK, D)] * 4
    scratch += [rows(PACK, D, F32), pltpu.VMEM((3, D, PACK), BF16), rows(4 * D, PACK)]
    scratch += [rows(tokens, 2 * D, F32), rows(tokens, 3 * D), rows(tokens, D, F32), rows(PACK, tokens)]
    scratch += [rows(tokens, PACK), rows(PACK, tokens, F32), rows(PACK, 128, F32), rows(PACK, D), rows(D, tokens)]
    scratch += [dma((11,)), dma((6,)), dma((10,))]
    return pl.pallas_call(
        middle_kernel,
        out_shape=[shape((1, 1), F32), shape((6, D), F32)] + out,
        in_specs=[hbm] * 16 + [vmem] * 5,
        out_specs=[vmem] * 2 + [hbm] * len(out),
        scratch_shapes=scratch,
        compiler_params=pltpu.CompilerParams(vmem_limit_bytes=63 * 1024 * 1024),
    )(*large, *small)


LEFT = 768
PIECES = ((Q_, 0, 1152), (E_, 0, 1280), (E_, 1280, 1280), (I_, 0, 1536), (D_, 0, 384), (O_, 0, 384))
Y_FIRST = (0, 1, 4)
TASKS = (
    0, 1, 96, 9, 4, 129, 97, 2, 103, 5, 99, 7, 8, 6, 101, 128, 102, 105,
    100, 132, 133, 64, 108, 12, 104, 136, 139, 134, 65, 15, 107, 111, 109, 137, 161, 13,
    160, 3, 131, 11, 141, 142, 70, 32, 68, 112, 110, 76, 140, 16, 168, 67, 144, 72,
    169, 75, 135, 71, 33, 36, 69, 143, 166, 173, 38, 98, 39, 43, 78, 130, 167, 73,
    37, 40, 79, 44, 34, 164, 46, 66, 77, 14, 47, 165, 45, 162, 171, 41, 172, 176,
    80, 138, 174, 74, 48, 10, 106, 42, 175, 35, 81, 145, 163, 170, 113, 17, 49, 177,
)


def reduce_kernel(*refs):
    given, (cols, norm_sums, loss, squares) = refs[0:11], refs[11:15]
    y_t, ge_t, glog, x_t, gqkv, mix_t, gattn, a_t, gh, act_t, gffn = given
    lane_olds, side_olds, moment = refs[15:21], refs[21:27], refs[27]
    outs, sums_out, totals_out = refs[28:33], refs[33], refs[34]
    own, side, first, second, column, fin = (refs[35 + 6 * i : 41 + 6 * i] for i in range(6))
    left, (glog_v, gqkv_v, gattn_v, gh_v, gffn_v), stage, tails, norm_t = refs[71:78], refs[78:83], refs[83], refs[84], refs[85]
    spread, spread_small = refs[86:89], refs[89:92]
    load_sem, ring_sem, tail_sem, side_recv, first_send, first_recv, second_send, second_recv = refs[92:100]
    z_send, z_recv, swap_send, swap_recv = refs[100:104]
    sems, small_sems = refs[104:110], refs[110:116]
    z, y, x, c = here()
    peers = all_peers()
    me = chip(z, y, x)

    barrier = pltpu.get_barrier_semaphore()
    greeted = [peers[XWAY], peers[YWAY], peers[SIDE], device(z, 1 - y, 1 - x, c)]
    greeted += [device((z + 1 + i) % 4, y, x, c) for i in range(3)]
    for peer in greeted:
        pl.semaphore_signal(barrier, inc=1, device_id=peer, device_id_type=MESH)

    tokens = cols.shape[0]

    def act_part(group):
        return act_t.at[pl.ds(LEFT * group, LEFT), 0:tokens]

    operands = (
        ((x_t, left[1]), (gqkv, gqkv_v)),
        ((y_t.at[:, 0:tokens], left[2]), (ge_t, left[3]), (glog.at[0:tokens, :], glog_v)),
        (),
        ((a_t.at[:, 0:tokens], left[0]), (gh.at[0:tokens, :], gh_v)),
        ((gffn.at[0:tokens, :], gffn_v), (act_part(0), left[5]), (act_part(1), left[6])),
        ((mix_t.at[:, 0:tokens], left[4]), (gattn.at[0:tokens, :], gattn_v)),
    )
    loads = {}
    waited = set()
    for task in TASKS:
        piece = task // 32 if task // 32 != 2 else 1
        if piece not in loads:
            loads[piece] = []
            for source, target in operands[piece]:
                number = sum(len(member) for member in loads.values())
                loads[piece].append(pltpu.make_async_copy(source, target, load_sem.at[number]))
                loads[piece][-1].start()

    def loaded(piece):
        piece = 1 if piece == 2 else piece
        if piece not in waited:
            waited.add(piece)
            for member in loads[piece]:
                member.wait()

    norm_t[...] = jnp.zeros(norm_t.shape, F32)
    norm_t[5:11, :] = norm_sums[...]
    pl.semaphore_wait(barrier, 7)

    def size_of(piece):
        return 2 * SHAPES[PIECES[piece][0]][0]

    def slot(ref, piece, index):
        size = size_of(piece)
        return ref[piece].at[pl.ds(pl.multiple_of(index * size, size), size), :]

    def half_of(piece):
        return SHAPES[PIECES[piece][0]][1] // 2

    def chosen(start):
        lane = lax.broadcasted_iota(jnp.int32, (1, TILE), 1) + start
        hit = (cols[:, 0:1] == lane) | (cols[:, 1:2] == lane)
        return jnp.where(hit, 1.0, 0.0).astype(BF16)

    def ring_copy(piece, rows, lanes, number, index):
        place = lax.rem(number, 3)
        return pltpu.make_async_remote_copy(
            src_ref=stage.at[place],
            dst_ref=side[piece].at[rows, lanes],
            send_sem=ring_sem.at[place],
            recv_sem=side_recv.at[piece, index],
            device_id=peers[SIDE],
            device_id_type=MESH,
        )

    def tail_copy(piece, rows, lanes, number, index):
        return pltpu.make_async_remote_copy(
            src_ref=tails.at[number],
            dst_ref=side[piece].at[rows, lanes],
            send_sem=tail_sem.at[number],
            recv_sem=side_recv.at[piece, index],
            device_id=peers[SIDE],
            device_id_type=MESH,
        )

    whole = pl.ds(0, LEFT)
    ring_count, tail_count = [0], [0]

    def give(piece, rows, lanes, number, index):
        def before():
            @pl.when(number >= 3)
            def _():
                ring_copy(piece, rows, lanes, number, index).wait_send()

        def write(value):
            stage[lax.rem(number, 3)] = value.astype(BF16)

        return before, write, lambda: ring_copy(piece, rows, lanes, number, index).start()

    def keep(piece, rows, lanes):
        def write(value):
            own[piece][rows, lanes] = value.astype(BF16)

        return lambda: None, write, lambda: None

    def plain(piece, mine, source, right, group):
        wide = PIECES[piece][2]
        half = c if mine else 1 - c
        rows = pl.ds(LEFT * group, LEFT)
        base = ring_count[0]

        def step(j):
            lanes = at(j, TILE)
            before, write, after = keep(piece, rows, lanes) if mine else give(
                piece, rows, lanes, base + j, group * (wide // TILE) + j
            )
            before()
            write(dot_nn(source[...], right[:, pl.ds(pl.multiple_of(half * wide + j * TILE, 128), TILE)]))
            after()

        each(wide // TILE, step)
        if not mine:
            ring_count[0] += wide // TILE
        if wide % TILE:
            start = wide - 128
            value = dot_nn(source[...], right[:, pl.ds(pl.multiple_of(half * wide + start, 128), 128)])
            if mine:
                own[piece][rows, start:wide] = value.astype(BF16)
            else:
                number = tail_count[0]
                tail_count[0] += 1
                groups = SHAPES[PIECES[piece][0]][0] // 24
                tails[number] = value.astype(BF16)
                tail_copy(piece, rows, pl.ds(start, 128), number, groups * (wide // TILE) + group).start()

    def wide_product(piece, mine):
        half = c if mine else 1 - c
        wide = half_of(piece)
        skip = PIECES[piece][1] // TILE
        base = ring_count[0]

        def both(j):
            start = pl.multiple_of(half * wide + (skip + j) * TILE, TILE)
            return dot_nn(left[2][...], glog_v[:, pl.ds(start, TILE)]) + dot_nn(left[3][...], chosen(start))

        def target(j):
            lanes = at(j, TILE)
            return keep(piece, whole, lanes) if mine else give(piece, whole, lanes, base + j, j)

        def step(j):
            before, write, after = target(j)
            before()
            write(both(j))
            after()

        if not mine:
            ring_count[0] += 5
        if skip == 0:
            each(5, step)
            return
        each(1, step)
        before, write, after = target(1)
        before()
        norm_part = jnp.where(half == 1, norm_t[...], 0.0).T
        write(both(1) + jnp.concatenate((norm_part, jnp.zeros((LEFT, TILE - 128), F32)), 1))
        after()
        for j in range(2, 5):
            before, write, after = target(j)
            before()

            @pl.when(half == 0)
            def _():
                write(both(j))

            @pl.when(half == 1)
            def _():
                if j == 2:
                    write(jnp.zeros((LEFT, TILE), F32))
                else:
                    write(dot_nn(left[3][...], chosen(half_of(piece) + (skip + j) * TILE)))

            after()

    def products(piece, mine):
        loaded(piece)
        if piece in (1, 2):
            wide_product(piece, mine)
        elif piece == 4:
            if not mine:
                for group in range(4):
                    source = left[5 + group % 2]
                    if group >= 2:
                        loads[piece][1 + group % 2].wait()
                    plain(piece, False, source, gffn_v, group)
                    plain(piece, True, source, gffn_v, group)
                    if group < 2:
                        again = pltpu.make_async_copy(act_part(group + 2), source, load_sem.at[12 + group])
                        again.start()
                        loads[piece][1 + group] = again
        else:
            source, right = {0: (left[1], gqkv_v), 3: (left[0], gh_v), 5: (left[4], gattn_v)}[piece]
            plain(piece, mine, source, right, 0)

    def combine(piece, target, parts):
        def some(rows, lanes):
            total = parts[0][rows, lanes].astype(F32)
            for member in parts[1:]:
                total = total + member[rows, lanes].astype(F32)
            target[rows, lanes] = total.astype(target.dtype)

        wide = PIECES[piece][2]
        if piece == 4:
            each(4, lambda group: some(at(group, 48), slice(0, wide)))
            return
        if wide >= 512:
            each(wide // 512, lambda j: some(slice(0, 48), at(j, 512)))
        if wide % 512:
            some(slice(0, 48), slice(wide // 512 * 512, wide))

    def hop(piece, k, land, index, sems, way):
        return pltpu.make_async_remote_copy(
            src_ref=slot(own, piece, k),
            dst_ref=slot(land, piece, index),
            send_sem=sems[0].at[piece, index],
            recv_sem=sems[1].at[piece, index],
            device_id=peers[way],
            device_id_type=MESH,
        )

    FIRST, SECOND = (first_send, first_recv), (second_send, second_recv)

    def landed(piece, land, index, sems):
        hop(piece, me, land, index, sems, XWAY).wait_recv()

    def block(piece, a, b, far):
        return chip(far, a, b) if piece in Y_FIRST else chip(far, b, a)

    def split(piece):
        return (y, x, YWAY, XWAY) if piece in Y_FIRST else (x, y, XWAY, YWAY)

    readied = set()

    def ready(piece):
        if piece in readied:
            return
        readied.add(piece)
        wide, groups = PIECES[piece][2], SHAPES[PIECES[piece][0]][0] // 24
        for group in range(groups):
            for j in range(wide // TILE):
                ring_copy(piece, pl.ds(LEFT * group, LEFT), at(j, TILE), 0, group * (wide // TILE) + j).wait_recv()
            if wide % TILE:
                index = groups * (wide // TILE) + group
                tail_copy(piece, pl.ds(LEFT * group, LEFT), pl.ds(wide - 128, 128), 0, index).wait_recv()

    def both_cores(piece, k):
        return (slot(own, piece, k), slot(side, piece, k))

    def first_block(piece, i):
        a, b, way, _ = split(piece)
        t, v = (z + i // 2) % 4, (1 - b) if i % 2 == 0 else b
        return block(piece, 1 - a, v, t), 2 * t + v, way

    def first_send_of(piece, i):
        ready(piece)
        k, index, way = first_block(piece, i)
        combine(piece, slot(own, piece, k), both_cores(piece, k))
        hop(piece, k, first, index, FIRST, way).start()

    def second_block(piece, i):
        a, b, _, way = split(piece)
        t = (z + i) % 4
        return block(piece, a, 1 - b, t), t, way

    def second_send_of(piece, i):
        k, t, way = second_block(piece, i)
        spot = 2 * t + 1 - split(piece)[1]
        landed(piece, first, spot, FIRST)
        combine(piece, slot(own, piece, k), both_cores(piece, k) + (slot(first, piece, spot),))
        hop(piece, k, second, t, SECOND, way).start()

    def z_copy(piece, i):
        t = (z + i) % 4
        return pltpu.make_async_remote_copy(
            src_ref=slot(own, piece, chip(t, y, x)),
            dst_ref=slot(column, piece, z),
            send_sem=z_send.at[piece, t],
            recv_sem=z_recv.at[piece, z],
            device_id=device(t, y, x, c),
            device_id_type=MESH,
        )

    def z_landed(piece, i):
        t = (z + i) % 4
        pltpu.make_async_remote_copy(
            src_ref=slot(own, piece, me),
            dst_ref=slot(column, piece, t),
            send_sem=z_send.at[piece, t],
            recv_sem=z_recv.at[piece, t],
            device_id=device(t, y, x, c),
            device_id_type=MESH,
        ).wait_recv()
        return slot(column, piece, t)

    def gathered(piece, t):
        spot = 2 * t + split(piece)[1]
        landed(piece, first, spot, FIRST)
        landed(piece, second, t, SECOND)
        return both_cores(piece, chip(t, y, x)) + (slot(first, piece, spot), slot(second, piece, t))

    def z_send_of(piece, i):
        t = (z + i) % 4
        combine(piece, slot(own, piece, chip(t, y, x)), gathered(piece, t))
        z_copy(piece, i).start()

    swaps = []

    def finish(piece):
        parts = gathered(piece, z)
        parts = parts + tuple(z_landed(piece, i) for i in (1, 2, 3))
        combine(piece, fin[piece], parts)
        m, skip, wide = PIECES[piece]
        size = SHAPES[m][0]
        lanes = pl.ds(pl.multiple_of(c * half_of(piece) + skip, 128), wide)
        swaps.append(
            pltpu.make_async_remote_copy(
                src_ref=fin[piece].at[pl.ds(pl.multiple_of((1 - c) * size, 8), size), :],
                dst_ref=outs[m].at[:, lanes],
                send_sem=swap_send.at[piece],
                recv_sem=swap_recv.at[piece],
                device_id=peers[SIDE],
                device_id_type=MESH,
            )
        )
        swaps[-1].start()
        outs[m][:, lanes] = fin[piece][pl.ds(pl.multiple_of(c * size, 8), size), :]

    for task in TASKS:
        piece, number = task // 32, task % 32
        if number < 2:
            products(piece, number == 1)
        elif number < 10:
            first_send_of(piece, number - 2)
        elif number < 14:
            second_send_of(piece, number - 10)
        elif number < 17:
            z_send_of(piece, number - 13)
        else:
            finish(piece)
    for piece in range(6):
        for i in range(8):
            k, index, way = first_block(piece, i)
            hop(piece, k, first, index, FIRST, way).wait_send()
        for i in range(4):
            k, t, way = second_block(piece, i)
            hop(piece, k, second, t, SECOND, way).wait_send()
        for i in (1, 2, 3):
            z_copy(piece, i).wait_send()
    for number in range(ring_count[0] - 3, ring_count[0]):
        ring_copy(1, whole, pl.ds(0, TILE), number, 0).wait_send()
    for number in range(tail_count[0]):
        tail_copy(1, whole, pl.ds(0, 128), number, 0).wait_send()
    for swap in swaps:
        swap.wait()

    sides, lanes, _, gs = statistics(outs, lane_olds, side_olds)
    scalars = lanes_of([jnp.sum(member, 0, keepdims=True) for member in sides] + [loss[...]])
    sums = jnp.concatenate(lanes + [scalars, squares[...]], 1)
    sums = sum_everywhere(sums, *spread, sems)
    sums_out[...] = sums
    updates = updates_of(sums, gs, sides, lane_olds, moment)[0]
    totals = lanes_of(
        [total_sum(update * update) for update in updates[:6]]
        + [jnp.sum(updates[6][i : i + 1] * updates[6][i : i + 1], 1, keepdims=True) for i in range(6)]
    )
    totals_out[...] = sum_everywhere(totals, *spread_small, small_sems)


def statistics(grads, lane_olds, side_olds):
    wide_g = grads[E_][...]
    gs = (wide_g[:, :VOCAB], wide_g[:, PLACE_AT:]) + tuple(grads[m][...] for m in (Q_, O_, I_, D_))
    gs = gs + (wide_g[:, 4096:4224],)
    decay = 1.0 - STEP ** (-0.8)
    sides, lanes = [], []
    wide_square = wide_g * wide_g + SQUARE_FLOOR
    squares = [wide_square[:, :VOCAB], wide_square[:, PLACE_AT:]] + [g * g + SQUARE_FLOOR for g in gs[2:6]]
    for index in range(6):
        mean = jnp.sum(squares[index], 1, keepdims=True) / squares[index].shape[1]
        sides.append(decay * column_of(as_row(side_olds[index])) + (1.0 - decay) * mean)
    lanes = [jnp.sum(square, 0, keepdims=True) for square in [wide_square] + squares[2:]]
    return sides, lanes, squares, gs


def updates_of(sums, gs, sides, lane_olds, moment):
    decay = 1.0 - STEP ** (-0.8)
    fresh = 1.0 - decay
    parts = [sums[:, :VOCAB], sums[:, PLACE_AT:WIDE]]
    parts += [sums[:, SUM_AT[i] : SUM_AT[i + 1]] for i in range(1, 5)]
    scalars = sums[:, SUM_AT[5] : SUM_AT[5] + 128]
    updates, lane_news = [], []
    for index in range(6):
        height = gs[index].shape[0] * 32
        lane_news.append(decay * as_row(lane_olds[index]) + fresh * (parts[index] / height))
        if index < 2:
            mean = jnp.sum(lane_news[index], 1, keepdims=True) / lane_news[index].shape[1]
        else:
            mean = lane_at(scalars, index) / height
        updates.append(gs[index] * lax.rsqrt(sides[index] * lane_news[index] / mean))
    norm_g = jnp.concatenate([row_of(lane_at(gs[6], NORM_AT - 4096 + i)) for i in range(6)], 0)
    moment_new = decay * moment[...] + fresh * (norm_g * norm_g + SQUARE_FLOOR)
    updates.append(norm_g * lax.rsqrt(moment_new))
    return updates, lane_news, norm_g, moment_new


def reduce_grads(large, small):
    tokens = 5 * SPAN
    vmem, hbm = pl.BlockSpec(memory_space=pltpu.VMEM), pl.BlockSpec(memory_space=pl.ANY)
    dma = pltpu.SemaphoreType.DMA
    scratch = []
    for count in (16, 16, 8, 4, 4):
        scratch += [pltpu.VMEM((count * 2 * SHAPES[m][0], wide), BF16) for m, _, wide in PIECES]
    scratch += [pltpu.VMEM((2 * SHAPES[m][0], wide), F32) for m, _, wide in PIECES]
    scratch += [pltpu.VMEM((LEFT, tokens), BF16)] * 7
    scratch += [pltpu.VMEM((tokens, width), BF16) for width in (TABLE_END, 3 * D, D, 4 * D, D)]
    scratch += [pltpu.VMEM((3, LEFT, TILE), BF16), pltpu.VMEM((6, LEFT, 128), BF16), pltpu.VMEM((128, D), F32)]
    scratch += [pltpu.VMEM((count, 1, SUMS), F32) for count in (2, 4, 4)]
    scratch += [pltpu.VMEM((count, 1, 128), F32) for count in (2, 4, 4)]
    scratch += [dma((14,)), dma((3,)), dma((6,)), dma((6, 10)), dma((6, 8)), dma((6, 8)), dma((6, 4)), dma((6, 4))]
    scratch += [dma((6, 4)), dma((6, 4)), dma((6,)), dma((6,))]
    scratch += ([dma] * 2 + [dma((3,))] * 4) * 2
    return pl.pallas_call(
        reduce_kernel,
        out_shape=[jax.ShapeDtypeStruct(shape, F32) for shape in SHAPES + ((1, SUMS), (1, 128))],
        in_specs=[hbm] * 11 + [vmem] * len(small),
        out_specs=[vmem] * 7,
        scratch_shapes=scratch,
        compiler_params=pltpu.CompilerParams(
            collective_id=1, has_side_effects=True, vmem_limit_bytes=63 * 1024 * 1024
        ),
    )(*large, *small)


def update_kernel(*refs):
    copies = [pltpu.make_async_copy(refs[i], refs[55 + i], refs[82].at[i]) for i in range(27)]
    for copy in copies:
        copy.start()
    for copy in copies:
        copy.wait()
    refs = refs[55:82] + refs[27:55]
    grads, sums, totals, ws, norms = refs[0:5], refs[5], refs[6], refs[7:13], refs[13]
    lane_olds, side_olds, moment = refs[14:20], refs[20:26], refs[26]
    loss_out, table_g, place_g, norm_g_out = refs[27:31]
    lane_outs, side_outs, moment_out, news, norm_new = refs[31:37], refs[37:43], refs[43], refs[44:50], refs[50]
    grad_outs = refs[51:55]
    sides, _, _, gs = statistics(grads, lane_olds, side_olds)
    updates, lane_news, norm_g, moment_new = updates_of(sums[...], gs, sides, lane_olds, moment)
    scalars = sums[:, SUM_AT[5] : SUM_AT[5] + 128]
    squares = sums[:, SUM_AT[5] + 128 :]
    loss_out[...] = lane_at(scalars, 6)
    table_g[...] = gs[0]
    place_g[...] = gs[1]
    norm_g_out[...] = norm_g
    moment_out[...] = moment_new
    for index in range(6):
        lane_outs[index][...] = lane_news[index].reshape(lane_outs[index].shape)
        side_outs[index][...] = row_of(sides[index]).reshape(side_outs[index].shape)
        if index >= 2:
            grad_outs[index - 2][...] = gs[index]
        entries = gs[index].shape[0] * gs[index].shape[1] * 32
        clip = jnp.maximum(1.0, jnp.sqrt(lane_at(totals[...], index) / entries))
        scale = learn_rate * jnp.sqrt(lane_at(squares, index) / entries) / clip
        news[index][...] = ws[index][...] - scale * updates[index]
    for i in range(6):
        clip = jnp.maximum(1.0, jnp.sqrt(lane_at(totals[...], 6 + i) / D))
        scale = learn_rate * jnp.sqrt(lane_at(squares, 6 + i) / D) / clip
        norm_new[i : i + 1, :] = norms[i : i + 1, :] - scale * updates[6][i : i + 1, :]


def update_weights(operands):
    lanes = (VOCAB, 512, 3 * D, D, 4 * D, D)
    held = (24, 24, 24, 24, 24, 96)
    shapes = [(1, 1), (24, VOCAB), (24, 512), (6, 24)]
    shapes += [(lane,) for lane in lanes] + [(size,) for size in held] + [(6, 24)]
    shapes += list(zip(held, lanes)) + [(6, 24)] + list(zip(held, lanes))[2:]
    return pl.pallas_call(
        update_kernel,
        out_shape=[jax.ShapeDtypeStruct(shape, F32) for shape in shapes],
        in_specs=[pl.BlockSpec(memory_space=pl.ANY)] * len(operands),
        out_specs=[pl.BlockSpec(memory_space=pltpu.VMEM)] * len(shapes),
        scratch_shapes=[pltpu.VMEM(member.shape, member.dtype) for member in operands]
        + [pltpu.SemaphoreType.DMA((len(operands),))],
        compiler_params=pltpu.CompilerParams(vmem_limit_bytes=63 * 1024 * 1024),
    )(*operands)


def norm_forward(value, gain, shift):
    centred = value - jnp.mean(value, -1, keepdims=True)
    inverse = lax.rsqrt(jnp.mean(centred * centred, -1, keepdims=True) + EPSILON)
    normed = centred * inverse
    return (normed * gain + shift, normed, inverse)


def norm_backward(grad_out, normed, inverse, gain):
    scaled = grad_out * gain
    back = inverse * (
        scaled
        - jnp.mean(scaled, -1, keepdims=True)
        - normed * jnp.mean(scaled * normed, -1, keepdims=True)
    )
    return (back, jnp.sum(grad_out * normed, 0), jnp.sum(grad_out, 0))


def mm(left, right, sides):
    return lax.dot_general(left, right, ((sides[:1], sides[1:]), ((), ())), preferred_element_type=F32)


def attend(qkv, allowed):
    by_head = qkv.reshape(qkv.shape[0], 3, HEADS, HEAD_DIM)
    query, key, value = by_head[:, 0], by_head[:, 1], by_head[:, 2]
    scores = jnp.einsum("qhe,khe->hqk", query, key, preferred_element_type=F32) * 0.125
    scores = jnp.where(allowed[None], scores, -1e30)
    highest = jnp.max(scores, -1, keepdims=True)
    raised = jnp.exp(scores - highest)
    summed = jnp.sum(raised, -1, keepdims=True)
    shares = (raised / summed).astype(BF16)
    mixture = jnp.einsum("hqk,khe->qhe", shares, value, preferred_element_type=F32)
    return mixture.astype(BF16).reshape(qkv.shape[0], D), highest + jnp.log(summed)


def attend_back(qkv, allowed, log_total, grad_mix):
    by_head = qkv.reshape(qkv.shape[0], 3, HEADS, HEAD_DIM)
    query, key, value = by_head[:, 0], by_head[:, 1], by_head[:, 2]
    grad_mix = grad_mix.reshape(qkv.shape[0], HEADS, HEAD_DIM)
    scores = jnp.einsum("qhe,khe->hqk", query, key, preferred_element_type=F32) * 0.125
    scores = jnp.where(allowed[None], scores, -1e30)
    shares = jnp.exp(scores - log_total)
    grad_share = jnp.einsum("qhe,khe->hqk", grad_mix, value, preferred_element_type=F32)
    grad_score = (shares * (grad_share - jnp.sum(shares * grad_share, -1, keepdims=True))).astype(BF16)
    grad_query = jnp.einsum("hqk,khe->qhe", grad_score, key, preferred_element_type=F32) * 0.125
    grad_key = jnp.einsum("hqk,qhe->khe", grad_score, query, preferred_element_type=F32) * 0.125
    grad_value = jnp.einsum("hqk,qhe->khe", shares.astype(BF16), grad_mix, preferred_element_type=F32)
    return jnp.stack((grad_query, grad_key, grad_value), 1).astype(BF16).reshape(qkv.shape)


def on_slice(token_arrays, lengths, weights, lane_olds, side_olds, moment):
    olds = lane_olds + side_olds + (moment,)
    found = front(token_arrays + weights, lengths)
    mask_count, gains, side, cols, keys, weight_sq = found[0:6]
    x_t, mix, a, act, y, slope, qkv_b, normed_a = found[6:14]
    normed_bc, (qkv_w, out_w, in_w, down_w, wide_w) = found[14:18], found[18:23]
    found = middle(
        (wide_w, qkv_w, out_w, in_w, down_w, y, act, a, mix, slope, qkv_b, normed_a) + tuple(normed_bc),
        (cols, keys, side, gains, mask_count),
    )
    loss_part, norm_sums = found[0:2]
    grad_logit, y_t, a_t, mix_t, act_t, ge_t, grad_ffn, grad_hidden, grad_attn, grad_qkv = found[2:]
    reduced = reduce_grads(
        (y_t, ge_t, grad_logit, x_t, grad_qkv, mix_t, grad_attn, a_t, grad_hidden, act_t, grad_ffn),
        (cols, norm_sums, loss_part, weight_sq) + olds,
    )
    found = update_weights(tuple(reduced) + weights + olds)
    grads = (None,) + tuple(found[24:28])
    mask_count = mask_count.reshape(())
    loss_sum, table_g, place_g, norm_g = found[0:4]
    lane_news = found[4:10]
    side_news = found[10:16]
    moment_new, norm_new = found[16], found[23]
    news = found[17:23]
    return (
        loss_sum.reshape(()),
        mask_count,
        table_g.T,
        place_g.T,
        grads[1],
        grads[2],
        grads[3],
        grads[4],
        norm_g.T,
        lane_news[0],
        side_news[0],
        lane_news[1],
        side_news[1],
        side_news[2],
        lane_news[2],
        side_news[3],
        lane_news[3],
        side_news[4],
        lane_news[4],
        side_news[5],
        lane_news[5],
        moment_new.T,
        news[0].T,
        news[1].T,
        news[2],
        news[3],
        news[4],
        news[5],
        norm_new.T,
    )


def on_device(
    whole_mesh,
    long_ids,
    long_targets,
    long_mask,
    long_lengths,
    short_ids,
    short_targets,
    short_mask,
    short_lengths,
    table,
    position,
    qkv_weight,
    out_weight,
    in_weight,
    down_weight,
    norms,
    table_rows,
    table_cols,
    position_rows,
    position_cols,
    qkv_rows,
    qkv_cols,
    out_rows,
    out_cols,
    in_rows,
    in_cols,
    down_rows,
    down_cols,
    norm_moment,
):
    if whole_mesh == (8, 4):
        return on_slice(
            (long_ids, long_targets, long_mask, short_ids, short_targets, short_mask),
            (long_lengths, short_lengths),
            (table.T, position.T, qkv_weight, out_weight, in_weight, down_weight, norms.T),
            (table_rows, position_rows, qkv_cols, out_cols, in_cols, down_cols),
            (table_cols, position_cols, qkv_rows, out_rows, in_rows, down_rows),
            norm_moment.T,
        )
    devices = lax.axis_size(("dp", "seq"))
    seq_index = lax.axis_index("seq")
    held = norms.shape[0]

    span = long_ids.shape[1]
    long_place = seq_index * span + lax.iota(jnp.int32, span)
    long_keep = (long_place[None, :] < long_lengths[:, None]).astype(jnp.int32)
    short_keep = (lax.iota(jnp.int32, SPAN)[None, :] < short_lengths[:, None]).astype(jnp.int32)
    long_pack = jnp.stack((long_ids, long_targets, long_mask * long_keep, long_keep), 1)
    short_pack = jnp.stack((short_ids, short_targets, short_mask * short_keep, short_keep), 1)
    moved = lax.all_to_all(
        jnp.concatenate((long_pack, short_pack[1:]), 0), "seq", split_axis=0, concat_axis=0, tiled=True
    )
    tokens = jnp.concatenate((moved, short_pack[:1]), 0)
    ids, targets, weight, keep = (tokens[:, i].reshape(-1) for i in range(4))
    weight = weight.astype(F32)
    count = tokens.shape[0] * span
    last = count - span
    alone = seq_index == lax.axis_size("seq") - 1
    token = lax.iota(jnp.int32, count)
    place = jnp.where(alone | (token >= last), token % span, token)
    row = jnp.where(alone | (token >= last), token // span, 0)
    allowed_long = (row[:last, None] == row[None, :last]) & (keep[None, :last] > 0)
    allowed_short = jnp.broadcast_to(keep[None, last:] > 0, (span, span))

    here_count = jnp.sum(long_pack[:, 2]) + jnp.sum(short_pack[:, 2])
    tall = table.T
    counts = jnp.broadcast_to(jnp.stack((here_count // 256, here_count % 256)).astype(F32)[None], (held, 2))
    wide_shard = jnp.concatenate(
        (tall, norms, counts, jnp.zeros((held, PLACE_AT - COUNT_AT - 2), F32), position.T), 1
    )
    shards = (wide_shard, qkv_weight, out_weight, in_weight, down_weight)
    wide_w, qkv_w, out_w, in_w, down_w = (
        lax.all_gather(shard.astype(BF16), ("dp", "seq"), axis=0, tiled=True) for shard in shards
    )
    column = lax.broadcasted_iota(jnp.int32, (1, WIDE), 1)
    chosen = ((ids[:, None] == column) | ((place[:, None] + PLACE_AT) == column)).astype(BF16)
    gains = wide_w[:, NORM_AT : NORM_AT + 6].astype(F32)
    sums = jnp.sum(wide_w[:, COUNT_AT : COUNT_AT + 2].astype(F32), 0)
    mask_count = (sums[0] * 256.0 + sums[1]) / held
    inverse_count = 1.0 / mask_count

    embedded = mm(chosen, wide_w, (1, 1))
    first, normed_a, inverse_a = norm_forward(embedded, gains[:, 0], gains[:, 1])
    first_b = first.astype(BF16)
    qkv_b = mm(first_b, qkv_w, (1, 0)).astype(BF16)
    mix_long, total_long = attend(qkv_b[:last], allowed_long)
    mix_short, total_short = attend(qkv_b[last:], allowed_short)
    mixture = jnp.concatenate((mix_long, mix_short), 0)
    second, normed_b, inverse_b = norm_forward(first + mm(mixture, out_w, (1, 0)), gains[:, 2], gains[:, 3])
    second_b = second.astype(BF16)
    hidden = mm(second_b, in_w, (1, 0))
    active, slope = gelu_pair(hidden)
    active_b = active.astype(BF16)
    third, normed_c, inverse_c = norm_forward(second + mm(active_b, down_w, (1, 0)), gains[:, 4], gains[:, 5])
    third_b = third.astype(BF16)
    logits = jnp.where(column < VOCAB, mm(third_b, wide_w, (1, 0)), -1e30)
    highest = jnp.max(logits, -1, keepdims=True)
    log_sum = highest + jnp.log(jnp.sum(jnp.exp(logits - highest), -1, keepdims=True))
    onehot = targets[:, None] == column
    picked = jnp.sum(jnp.where(onehot, logits, 0.0), -1)
    loss_part = jnp.sum(weight * (log_sum[:, 0] - picked))
    grad_logit = (
        (jnp.exp(logits - log_sum) - onehot.astype(F32)) * (weight * inverse_count)[:, None]
    ).astype(BF16)
    grad_third = mm(grad_logit, wide_w, (1, 1))
    grad_second, gain_c, shift_c = norm_backward(grad_third, normed_c, inverse_c, gains[:, 4])
    grad_ffn = grad_second.astype(BF16)
    down_grad = mm(active_b, grad_ffn, (0, 0)).astype(BF16)
    grad_hidden = (mm(grad_ffn, down_w, (1, 1)) * slope).astype(BF16)
    in_grad = mm(second_b, grad_hidden, (0, 0)).astype(BF16)
    grad_second = grad_second + mm(grad_hidden, in_w, (1, 1))
    grad_first, gain_b, shift_b = norm_backward(grad_second, normed_b, inverse_b, gains[:, 2])
    grad_attn = grad_first.astype(BF16)
    out_grad = mm(mixture, grad_attn, (0, 0)).astype(BF16)
    grad_mix = mm(grad_attn, out_w, (1, 1)).astype(BF16)
    grad_qkv = jnp.concatenate(
        (
            attend_back(qkv_b[:last], allowed_long, total_long, grad_mix[:last]),
            attend_back(qkv_b[last:], allowed_short, total_short, grad_mix[last:]),
        ),
        0,
    )
    qkv_grad = mm(first_b, grad_qkv, (0, 0)).astype(BF16)
    grad_first = grad_first + mm(grad_qkv, qkv_w, (1, 1))
    grad_embed, gain_a, shift_a = norm_backward(grad_first, normed_a, inverse_a, gains[:, 0])
    wide_grad = mm(
        jnp.concatenate((third_b, grad_embed.astype(BF16)), 0),
        jnp.concatenate((grad_logit, chosen), 0),
        (0, 0),
    )
    norm_part = jnp.stack((gain_a, shift_a, gain_b, shift_b, gain_c, shift_c), 1)
    wide_grad = lax.dynamic_update_slice(wide_grad.astype(BF16), norm_part.astype(BF16), (0, NORM_AT))
    grads = (wide_grad, qkv_grad, out_grad, in_grad, down_grad)
    wide_g, qkv_g, out_g, in_g, down_g = (
        lax.psum_scatter(grad.astype(F32), ("dp", "seq"), scatter_dimension=0, tiled=True) for grad in grads
    )
    table_g, place_g = wide_g[:, :VOCAB], wide_g[:, PLACE_AT:]
    norm_g = wide_g[:, NORM_AT : NORM_AT + 6]

    decay = 1.0 - STEP ** (-0.8)
    matrices = (
        (qkv_weight, qkv_g, qkv_rows, qkv_cols),
        (out_weight, out_g, out_rows, out_cols),
        (in_weight, in_g, in_rows, in_cols),
        (down_weight, down_g, down_rows, down_cols),
    )
    wide = (
        (tall, table_g, table_cols, table_rows),
        (position.T, place_g, position_cols, position_rows),
    )
    row_news = [
        decay * member[2] + (1.0 - decay) * jnp.mean(member[1] * member[1] + SQUARE_FLOOR, 1)
        for member in matrices + wide
    ]
    col_parts = [jnp.sum(member[1] * member[1] + SQUARE_FLOOR, 0) for member in matrices + wide]
    row_totals = jnp.stack([jnp.sum(rows_new) for rows_new in row_news])
    weight_sq = jnp.stack([jnp.sum(member[0] * member[0]) for member in matrices + wide])
    stats = lax.psum(
        col_parts + [row_totals, weight_sq, jnp.sum(norms * norms, 0), loss_part.reshape(1)], ("dp", "seq")
    )
    updates = []
    cols_out = []
    for index, member in enumerate(matrices + wide):
        full_rows = member[0].shape[0] * devices
        cols_new = decay * member[3] + (1.0 - decay) * stats[index] / full_rows
        if index < 4:
            mean = stats[6][index] / full_rows
        else:
            mean = jnp.mean(cols_new)
        updates.append(member[1] * lax.rsqrt(row_news[index][:, None] * cols_new[None, :] / mean))
        cols_out.append(cols_new)
    moment_new = decay * norm_moment + (1.0 - decay) * (norm_g * norm_g + SQUARE_FLOOR)
    norm_update = norm_g * lax.rsqrt(moment_new)
    update_sq = jnp.stack([jnp.sum(update * update) for update in updates])
    totals = lax.psum((update_sq, jnp.sum(norm_update * norm_update, 0)), ("dp", "seq"))
    news = []
    for index, member in enumerate(matrices + wide):
        entries = member[0].shape[0] * member[0].shape[1] * devices
        clip = jnp.maximum(1.0, jnp.sqrt(totals[0][index] / entries))
        news.append(
            member[0] - learn_rate * jnp.sqrt(stats[7][index] / entries) * updates[index] / clip
        )
    norm_rows = norms.shape[0] * devices
    norm_clip = jnp.maximum(1.0, jnp.sqrt(totals[1] / norm_rows))
    norm_new = norms - learn_rate * jnp.sqrt(stats[8] / norm_rows) * norm_update / norm_clip
    return (
        stats[9][0],
        mask_count,
        table_g.T,
        place_g.T,
        qkv_g,
        out_g,
        in_g,
        down_g,
        norm_g,
        cols_out[4],
        row_news[4],
        cols_out[5],
        row_news[5],
        row_news[0],
        cols_out[0],
        row_news[1],
        cols_out[1],
        row_news[2],
        cols_out[2],
        row_news[3],
        cols_out[3],
        moment_new,
        news[4].T,
        news[5].T,
        news[0],
        news[1],
        news[2],
        news[3],
        norm_new,
    )


def solution(mesh):
    split, wide = P(("dp", "seq"), None), P(None, ("dp", "seq"))
    shard, same = P(("dp", "seq")), P()
    return jax.shard_map(
        functools.partial(on_device, (mesh.shape["dp"], mesh.shape["seq"])),
        mesh=mesh,
        in_specs=(P("dp", "seq"),) * 3
        + (P("dp"),)
        + (split,) * 3
        + (shard,)
        + (wide,) * 2
        + (split,) * 5
        + (same, shard) * 2
        + (shard, same) * 4
        + (split,),
        out_specs=(same, same)
        + (wide,) * 2
        + (split,) * 5
        + (same, shard) * 2
        + (shard, same) * 4
        + (split,)
        + (wide,) * 2
        + (split,) * 5,
        check_vma=False,
    )
```

profile of v0, /device:TPU:0, one launch (start us, length us, event | category | flops | bytes accessed | tf_op | source)
XLA Modules:
  0.0 317.4 jit_solution(7385921520052929092)
XLA Ops:
  0.7 121.0 %shard_map.491 = (f32[1,1]{1,0:T(1,128)}, f32[16,768]{1,0:T(8,128)}, f32[640,128]{1,0:T(8,128)}, s32[640,128]{1,0:T(8,128)}, s32[8,640]{1,0:T(8,128)}, /*index=5...) custom-call(s32[3,128]{1,0:T(4,128)} %refs_0_.1, ...), custom_call_target="tpu_custom_call" | custom-call | tf_op jit(solution)/shard_map/pallas_call | solution.py:621
  121.7 57.7 %shard_map.492 = (f32[1,1]{1,0:T(1,128)}, f32[6,768]{1,0:T(8,128)}, bf16[768,4352]{1,0:T(8,128)(2,1)}, bf16[768,768]{1,0:T(8,128)(2,1)}, bf16[768,768]{1,0:T(8,1...) custom-call(bf16[768,5120]{1,0:T(8,128)(2,1)} %get-tuple-element.99., ...), custom_call_target="tpu_custom_call" | custom-call | tf_op jit(solution)/shard_map/pallas_call | solution.py:950
  179.3 132.1 %shard_map.493 = (f32[24,5120]{1,0:T(8,128)}, f32[24,2304]{1,0:T(8,128)}, f32[24,768]{1,0:T(8,128)}, f32[24,3072]{1,0:T(8,128)}, f32[96,768]{1,0:T(8,128)}, /*index=5*/f32[1,12288]{1,0:T(1,128)}, f32[1,128]{1,0:T(1,128)}) custom-call(bf16[768,768]{1,0:T(8,128)(2,1)} %get-tuple-element.120.refs_0_, bf16[768,640]{1,0:T(8,128)(2,1)} %get-tuple-element.121.refs_1_, ...), custom_call_target="tpu_custom_call" | custom-call | tf_op jit(solution)/shard_map/pallas_call | solution.py:1409
  311.4 3.9 %shard_map.494 = (f32[1,1]{1,0:T(1,128)}, f32[24,4101]{1,0:T(8,128)}, f32[24,512]{1,0:T(8,128)}, f32[6,24]{1,0:T(8,128)}, f32[4101]{0:T(1024)}, /*index=5*/f32[5...) custom-call(f32[24,5120]{1,0:T(8,128)} %get-tuple-element.134.refs_0, ...), custom_call_target="tpu_custom_call" | custom-call | tf_op jit(solution)/shard_map/pallas_call | solution.py:1463
where the time goes:
time: 322 us; the launch traced here: 317 us
  Pallas kernels  315 us (98%)
    pallas_call x1, Pallas kernels, reduce_grads(): pl.pallas_call(reduce_kernel, out_shape=[jax.ShapeDtypeStruct(shape, F32)...  132 us
    pallas_call x1, Pallas kernels, front(): pl.pallas_call(front_kernel, out_shape=small + out, in_specs=[hbm] * 13 +...  121 us
    pallas_call x1, Pallas kernels, middle(): pl.pallas_call(middle_kernel, out_shape=[shape((1, 1), F32), shape((6, D)...  57.7 us

commit v1 on v0

--- a/solution.py
+++ b/solution.py
@@ -422,7 +422,7 @@
         spot = (lane + shift + PLACE_AT).astype(F32)
         row_lane = (lane * 0 + row).astype(F32)
         ids, targets, weight = (tile[i : i + 1].astype(F32) for i in (0, 2, 3))
-        stacked = jnp.concatenate((ids, spot, targets, weight, row_lane, zeros, zeros, zeros), 0)
+        stacked = jnp.concatenate((ids, spot, targets, weight, row_lane, tile[5:6].astype(F32), zeros, zeros), 0)
         stacked = jnp.concatenate((stacked, jnp.zeros((120, SPAN), F32)), 0)
         cols[b * SPAN : (b + 1) * SPAN, :] = stacked.T.astype(jnp.int32)
         keys[0:1, b * SPAN : (b + 1) * SPAN] = tile[5:6]
@@ -666,17 +666,15 @@
     nb, nc = refs[40:42], refs[42:44]
     slope_ring, act_ring, down_ring = refs[44:47]
     logits, glog, gh, gffn, gattn, gatt, packed, grad, turned, act_turned = refs[47:57]
-    back_kv, gqkv, whole_grad, pick, pick_t, bias, side_pack, dq, ge = refs[57:66]
-    load_sem, ring_sem, out_sem = refs[66:69]
+    back_kv, gqkv, whole_grad, pick, pick_t, bias, side_pack, side_turned, dq, ge = refs[57:67]
+    load_sem, ring_sem, out_sem = refs[67:70]
     tokens = cols.shape[0]
     names = ("wide", "y", "nc0", "nc1", "in_w", "nb0", "nb1", "out_w", "qkv", "qkv_w", "na")
     sources = (wide_h, y_h, nc_h[0], nc_h[1], in_wh, nb_h[0], nb_h[1], out_wh, qkv_h, qkv_wh, na_h)
     targets = (wide, plain, nc[0], nc[1], in_w, nb[0], nb[1], out_w, qkv, qkv_w, na)
-    loads = {}
-    for i, name in enumerate(names):
-        if name != "y":
-            loads[name] = pltpu.make_async_copy(sources[i], targets[i], load_sem.at[i])
-            loads[name].start()
+    loads = {name: pltpu.make_async_copy(sources[i], targets[i], load_sem.at[i]) for i, name in enumerate(names)}
+    for name in ("y", "wide"):
+        loads[name].start()
 
     weight_row = keys[3:4, :].astype(F32)
     weight_col = cols[:, 3:4].astype(F32)
@@ -737,26 +735,26 @@
     def wait_load(name):
         loads[name].wait()
 
-    load_plain(y_h).start()
-    for name in names:
-        if name in ("wide", "nc0", "nc1"):
-            wait_load(name)
+    wait_load("wide")
+    for name in names[2:]:
+        loads[name].start()
 
     def block_step(block, carry):
         slot_col = lax.broadcasted_iota(jnp.int32, (PACK, 1), 0).astype(F32) + (block * PACK).astype(F32)
         slot_row = lax.broadcasted_iota(jnp.int32, (1, PACK), 1).astype(F32) + (block * PACK).astype(F32)
         hit = jnp.where(rank_row == slot_col, 1.0, 0.0)
         pick[...] = hit.astype(BF16)
-        pick_t[...] = jnp.where(rank_col == slot_row, 1.0, 0.0).astype(BF16)
+        hit_t = jnp.where(rank_col == slot_row, 1.0, 0.0)
+        pick_t[...] = hit_t.astype(BF16)
         target = jnp.sum(hit * keys[2:3, :].astype(F32), 1, keepdims=True)
-        row_of_token = jnp.sum(hit * keys[1:2, :].astype(F32), 1, keepdims=True)
         weight = jnp.sum(hit, 1, keepdims=True)
-        bias[...] = jnp.where(
-            (row_of_token == keys[1:2, :].astype(F32)) & (keys[0:1, :] > 0), 0.0, -1e30
-        )
+        row_col = cols[:, 4:5].astype(F32)
+        row_of_token = jnp.sum(hit_t * row_col, 0, keepdims=True)
+        bias[...] = jnp.where((row_of_token == row_col) & (cols[:, 5:6] > 0), 0.0, -1e30)
         side_pack[...] = (
             dot_nn(pick[...], side_first) + dot_nn(pick[...], side_second) + dot_nn(pick[...], side_third)
         )
+        side_turned[...] = side_pack[...].T
         for kind in range(3):
             for j in range(2):
                 rings[kind](j).start()
@@ -796,6 +794,12 @@
         out_copy(0, block).start()
         for index in range(D // TILE):
             grad[:, at(index, TILE)] = dot_nt(glog[...], wide[at(index, TILE), 0:TABLE_END])
+
+        @pl.when(block == 0)
+        def _():
+            for name in names[2:4]:
+                wait_load(name)
+
         normed = dot_nn(pick[...], nc[0][...]) + dot_nn(pick[...], nc[1][...])
         found = grad[...]
         back = layer_norm_back(found, normed, lane_at(side_pack[...], 14), norm_rows[4])
@@ -854,31 +858,33 @@
             query = dot_nn(pick[...], qkv[:, spots[0]]).astype(BF16)
             key, val = qkv[:, spots[1]], qkv[:, spots[2]]
             given = gatt[:, at(pair, 128)]
+            key_t = key.T
             found = []
             for first in (True, False):
                 lanes_here = head_lanes(first)
                 chosen = jnp.where(lanes_here, query, jnp.zeros_like(query))
                 mine = jnp.where(lanes_here, given, jnp.zeros_like(given))
-                total = lane_at(side_pack[...], 2 * pair + (0 if first else 1))
-                shares = jnp.exp(dot_nt(chosen, key) * 0.125 + bias[...] - total)
-                grad_share = dot_nt(mine, val)
-                middle = jnp.sum(shares * grad_share, 1, keepdims=True)
+                total = side_turned[pl.ds(2 * pair + (0 if first else 1), 1), :]
+                shares = jnp.exp(dot_nt(key, chosen) * 0.125 + bias[...] - total)
+                grad_share = dot_nt(val, mine)
+                middle = jnp.sum(shares * grad_share, 0, keepdims=True)
                 grad_score = (shares * (grad_share - middle)).astype(BF16)
                 found.append(
                     (
-                        dot_nn(grad_score, key) * 0.125,
-                        dot_tn(grad_score, query) * 0.125,
-                        dot_tn(shares.astype(BF16), given),
+                        dot_nn(key_t, grad_score) * 0.125,
+                        dot_nn(grad_score, query) * 0.125,
+                        dot_nn(shares.astype(BF16), given),
                     )
                 )
             lanes_here = head_lanes(True)
-            dq[:, at(pair, 128)] = jnp.where(lanes_here, found[0][0], found[1][0]).astype(BF16)
+            both = jnp.concatenate((found[0][0][0:HEAD_DIM], found[1][0][HEAD_DIM:]), 0)
+            dq[at(pair, 128), :] = both.astype(BF16)
             for i in (1, 2):
                 spot = pl.ds(pl.multiple_of((i - 1) * D + pair * 128, 128), 128)
                 back_kv[:, spot] = back_kv[:, spot] + jnp.where(lanes_here, found[0][i], found[1][i])
 
         each(HEADS // 2, attend_pair_back)
-        gqkv[:, 0:D] = (gqkv[:, 0:D].astype(F32) + dot_nn(pick_t[...], dq[...])).astype(BF16)
+        gqkv[:, 0:D] = (gqkv[:, 0:D].astype(F32) + dot_nt(pick_t[...], dq[...])).astype(BF16)
         for i in range(len(outs)):
             out_copy(i, block).wait()
         return carry
@@ -945,7 +951,8 @@
     scratch += [rows(PACK, TABLE_END, F32), rows(PACK, TABLE_END), rows(PACK, 4 * D)] + [rows(PACK, D)] * 4
     scratch += [rows(PACK, D, F32), pltpu.VMEM((3, D, PACK), BF16), rows(4 * D, PACK)]
     scratch += [rows(tokens, 2 * D, F32), rows(tokens, 3 * D), rows(tokens, D, F32), rows(PACK, tokens)]
-    scratch += [rows(tokens, PACK), rows(PACK, tokens, F32), rows(PACK, 128, F32), rows(PACK, D), rows(D, tokens)]
+    scratch += [rows(tokens, PACK), rows(tokens, PACK, F32), rows(PACK, 128, F32), rows(128, PACK, F32)]
+    scratch += [rows(D, PACK), rows(D, tokens)]
     scratch += [dma((11,)), dma((6,)), dma((10,))]
     return pl.pallas_call(
         middle_kernel,

time: 322 us -> 321 us (level)
  no operation moved by 1% of the time
where the time goes in v1:
time: 321 us; the launch traced here: 318 us
  Pallas kernels  315 us (98%)
    pallas_call x1, Pallas kernels, reduce_grads(): pl.pallas_call(reduce_kernel, out_shape=[jax.ShapeDtypeStruct(shape, F32)...  132 us
    pallas_call x1, Pallas kernels, front(): pl.pallas_call(front_kernel, out_shape=small + out, in_specs=[hbm] * 13 +...  121 us
    pallas_call x1, Pallas kernels, middle(): pl.pallas_call(middle_kernel, out_shape=[shape((1, 1), F32), shape((6, D)...  58.2 us

profile of v1, /device:TPU:0, one launch (start us, length us, event | category | flops | bytes accessed | tf_op | source)
XLA Modules:
  0.0 317.9 jit_solution(13376906385705954660)
XLA Ops:
  0.7 121.0 %shard_map.491 = (f32[1,1]{1,0:T(1,128)}, f32[16,768]{1,0:T(8,128)}, f32[640,128]{1,0:T(8,128)}, s32[640,128]{1,0:T(8,128)}, s32[8,640]{1,0:T(8,128)}, /*index=5...) custom-call(s32[3,128]{1,0:T(4,128)} %refs_0_.1, ...), custom_call_target="tpu_custom_call" | custom-call | tf_op jit(solution)/shard_map/pallas_call | solution.py:621
  121.7 58.2 %shard_map.492 = (f32[1,1]{1,0:T(1,128)}, f32[6,768]{1,0:T(8,128)}, bf16[768,4352]{1,0:T(8,128)(2,1)}, bf16[768,768]{1,0:T(8,128)(2,1)}, bf16[768,768]{1,0:T(8,1...) custom-call(bf16[768,5120]{1,0:T(8,128)(2,1)} %get-tuple-element.99., ...), custom_call_target="tpu_custom_call" | custom-call | tf_op jit(solution)/shard_map/pallas_call | solution.py:957
  179.9 132.1 %shard_map.493 = (f32[24,5120]{1,0:T(8,128)}, f32[24,2304]{1,0:T(8,128)}, f32[24,768]{1,0:T(8,128)}, f32[24,3072]{1,0:T(8,128)}, f32[96,768]{1,0:T(8,128)}, /*index=5*/f32[1,12288]{1,0:T(1,128)}, f32[1,128]{1,0:T(1,128)}) custom-call(bf16[768,768]{1,0:T(8,128)(2,1)} %get-tuple-element.120.refs_0_, bf16[768,640]{1,0:T(8,128)(2,1)} %get-tuple-element.121.refs_1_, ...), custom_call_target="tpu_custom_call" | custom-call | tf_op jit(solution)/shard_map/pallas_call | solution.py:1416
  312.0 3.9 %shard_map.494 = (f32[1,1]{1,0:T(1,128)}, f32[24,4101]{1,0:T(8,128)}, f32[24,512]{1,0:T(8,128)}, f32[6,24]{1,0:T(8,128)}, f32[4101]{0:T(1024)}, /*index=5*/f32[5...) custom-call(f32[24,5120]{1,0:T(8,128)} %get-tuple-element.134.refs_0, ...), custom_call_target="tpu_custom_call" | custom-call | tf_op jit(solution)/shard_map/pallas_call | solution.py:1470
